TPU v7x, 256 devices: a whole 4x4x8 slice. The times are simulated.
256 devices in a mesh: ctx: 64 (over y_lo, x, z), hid: 4 (over y_hi, core).
Axes of the slice: x: 4, y: 4 (y_hi: 2, y_lo: 2; y = y_hi * 2 + y_lo), z: 8, core: 2. Of those that a mesh axis runs over, the one named last changes fastest.
Arguments:
- activations: bfloat16 [16384, 4096], P('ctx'), may hold values from -6 to 6
- w_in: bfloat16 [3, 4096, 4096], P(None, 'ctx', 'hid'), may hold values from -0.09375 to 0.09375
- short_taps: float32 [3, 4096, 3], P(None, 'hid'), may hold values from -3 to 3
- long_filter: float32 [4096, 16384], P('hid', 'ctx')
- w_out: bfloat16 [4096, 4096], P('hid'), may hold values from -0.09375 to 0.09375
Outputs:
- layer_out: bfloat16 [16384, 4096], P('ctx', 'hid')
All inputs are finite; a program needn't handle non-finite values.
Results may differ from a plain program's by a relative error of at most 0.015.
Values may be sent and summed in bfloat16 or wider, within the bound.
A program may use at most 128 MiB of HBM per device.

v0:
```python
import math

import jax
import jax.numpy as jnp
from jax import lax
from jax.sharding import PartitionSpec as P

TAPS = 3


HIGH = lax.Precision.HIGHEST


def shifted(array, axis, by):
    devices = lax.axis_size(axis)
    pairs = [(i, i + by) for i in range(devices) if 0 <= i + by < devices]
    return lax.ppermute(array, axis, pairs)


def phase_table(rows, cols, period, offset):
    row_ids = lax.broadcasted_iota(jnp.int32, (rows, cols), 0)
    col_ids = lax.broadcasted_iota(jnp.int32, (rows, cols), 1) + offset
    angle = (row_ids * col_ids % period).astype(jnp.float32) * (2.0 * math.pi / period)
    return (jnp.cos(angle), jnp.sin(angle))


def spectrum_of(values, period):
    cosine, sine = phase_table(values.shape[-1], period, period, 0)
    real = jnp.einsum("...n,nf->...f", values, cosine, precision=HIGH)
    imag = -jnp.einsum("...n,nf->...f", values, sine, precision=HIGH)
    return (real, imag)


def upper_half(real, imag):
    period = real.shape[-1]
    half = period // 2
    cosine, sine = phase_table(period, half, period, half)
    first = jnp.einsum("...f,fi->...i", real, cosine, precision=HIGH)
    second = jnp.einsum("...f,fi->...i", imag, sine, precision=HIGH)
    return (first - second) / period


def block_convolve(lag_re, lag_im, sig_re, sig_im):
    count = sig_re.shape[0]
    period = 2 * count
    cosine, sine = phase_table(period, count, period, 0)

    def ahead(real, imag):
        out_re = jnp.einsum("kd,d...->k...", cosine, real, precision=HIGH) + jnp.einsum(
            "kd,d...->k...", sine, imag, precision=HIGH
        )
        out_im = jnp.einsum("kd,d...->k...", cosine, imag, precision=HIGH) - jnp.einsum(
            "kd,d...->k...", sine, real, precision=HIGH
        )
        return (out_re, out_im)

    lag_fr, lag_fi = ahead(lag_re, lag_im)
    sig_fr, sig_fi = ahead(sig_re, sig_im)
    prod_re = lag_fr * sig_fr - lag_fi * sig_fi
    prod_im = lag_fr * sig_fi + lag_fi * sig_fr
    back_cos, back_sin = phase_table(count, period, period, 0)
    res_re = (
        jnp.einsum("ck,k...->c...", back_cos, prod_re, precision=HIGH)
        - jnp.einsum("ck,k...->c...", back_sin, prod_im, precision=HIGH)
    ) / period
    res_im = (
        jnp.einsum("ck,k...->c...", back_cos, prod_im, precision=HIGH)
        + jnp.einsum("ck,k...->c...", back_sin, prod_re, precision=HIGH)
    ) / period
    return (res_re, res_im)


def on_device(activations, w_in, short_taps, long_filter, w_out):
    blocks = lax.axis_size("ctx")
    length = activations.shape[0]
    local_width = w_in.shape[2]
    columns = activations
    summed = jnp.einsum(
        "td,jdc->cjt",
        columns,
        lax.all_gather(w_in, "ctx", axis=1, tiled=True),
        preferred_element_type=jnp.float32,
    )
    branches = summed.astype(jnp.bfloat16)
    rim_rows = branches[:, :, length - (TAPS - 1) :]
    earlier = shifted(rim_rows, "ctx", 1)
    extended = jnp.concatenate([earlier, branches], axis=2).astype(jnp.float32)
    tap_table = jnp.transpose(short_taps, (1, 0, 2))
    filtered = jnp.zeros((local_width, 3, length), jnp.float32)
    for lag in range(TAPS):
        begin = TAPS - 1 - lag
        filtered = (
            filtered + tap_table[:, :, lag : lag + 1] * extended[:, :, begin : begin + length]
        )
    driven = filtered[:, 0] * filtered[:, 2]
    stacked = jnp.stack([driven, long_filter]).reshape(2, 1, blocks, local_width // blocks, length)
    piece = lax.all_to_all(stacked, "ctx", split_axis=2, concat_axis=1, tiled=True)
    signal = piece[0, :, 0]
    filter_rows = piece[1, :, 0]
    prior = jnp.concatenate([jnp.zeros_like(filter_rows[:1]), filter_rows[:-1]], axis=0)
    lagged = jnp.concatenate([prior, filter_rows], axis=-1)
    sig_re, sig_im = spectrum_of(signal, 2 * length)
    lag_re, lag_im = spectrum_of(lagged, 2 * length)
    res_re, res_im = block_convolve(lag_re, lag_im, sig_re, sig_im)
    result = upper_half(res_re, res_im)
    returned = result.reshape(blocks, 1, result.shape[1], length)
    merged = lax.all_to_all(returned, "ctx", split_axis=0, concat_axis=1, tiled=True)
    convolved = merged.reshape(local_width, length)
    gated = (filtered[:, 1] * convolved).astype(jnp.bfloat16)
    columns = w_out
    result = lax.psum_scatter(
        jnp.einsum("cd,ct->dt", columns, gated, preferred_element_type=jnp.float32).astype(
            jnp.bfloat16
        ),
        "hid",
        scatter_dimension=0,
        tiled=True,
    ).astype(jnp.float32)
    return result.T.astype(jnp.bfloat16)


def solution(mesh):
    return jax.shard_map(
        on_device,
        mesh=mesh,
        in_specs=(
            P("ctx", None),
            P(None, "ctx", "hid"),
            P(None, "hid", None),
            P("hid", "ctx"),
            P("hid", None),
        ),
        out_specs=P("ctx", "hid"),
        check_vma=False,
    )
```

profile of v0, /device:TPU:1, one launch (start us, length us, event | category | flops | bytes accessed | tf_op | source)
XLA Modules:
  0.0 582.9 jit_solution(3135271495761747623)
XLA Ops:
  7.3 0.9 fusion.189
  8.2 318.3 %all-gather.2.cloned.1.call-done = bf16[3,4096,1024]{2,1,0:T(8,128)(2,1)} async-done(((bf16[3,64,1024]{2,1,0:T(8,128)(2,1)}), bf16[3,4096,1024]{2,1,0:T(8,128)(2,1)}) %all-gather.2.cloned.1.call-update) | async-done | bytes 25165840 | tf_op jit(solution)/shard_map/all_gather | solution.py:81
  326.5 11.8 %fusion.20 = bf16[1024,3,256]{0,2,1:T(8,128)(2,1)S(1)} fusion(bf16[3,4096,1024]{2,1,0:T(8,128)(2,1)} %all-gather.2.cloned.1.call-done, bf16[256,4096]{1,0:T(8,128)(2,1)S(1)} %copy-done), kind=kOutput, calls=%fused_computation.39 | convolution fusion | flops 6443237376 | bytes 28835840 | tf_op jit(solution)/shard_map/td,jdc->cjt/dot_general | solution.py:78
  338.3 1.3 collective-permute-start
  339.7 0.8 collective-permute-done
  340.9 0.9 fusion.1
  341.9 1.6 copy-done.2
  344.9 1.5 copy.27
  346.4 7.9 %all-to-all-start = ((f32[2,1,64,16,256]{4,3,1,0,2:T(8,128)}), f32[2,1,64,16,256]{4,3,1,0,2:T(8,128)S(1)}, u32[]{:S(2)}, u32[]{:S(2)}) async-start(f32[2,1,64,16,256]{4,3,1,0,2:T(8,128)} %copy.27), calls=%async_computation | async-start | bytes 4194304 | tf_op jit(solution)/shard_map/all_to_all | solution.py:97
  354.6 28.8 %all-to-all-done = f32[2,1,64,16,256]{4,3,1,0,2:T(8,128)S(1)} async-done(((f32[2,1,64,16,256]{4,3,1,0,2:T(8,128)}), f32[2,1,64,16,256]{4,3,1,0,2:T(8,128)S(1)}, u32[]{:S(2)}, u32[]{:S(2)}) %all-to-all-start) | async-done | bytes 2097184 | tf_op jit(solution)/shard_map/all_to_all | solution.py:97
  383.7 0.9 copy-done.3
  384.8 7.3 %convolution_negate_fusion.1 = f32[64,16,512]{2,1,0:T(8,128)S(1)} fusion(f32[63,16,256]{2,1,0:T(8,128)S(1)} %slice_bitcast_fusion.2, f32[64,16,256]{2,1,0:T(8,128)S(1)} %get-tuple-element.9), kind=kOutput, calls=%fused_computation.34 | convolution fusion | flops 3226992640 | bytes 4177920 | tf_op jit(solution)/shard_map/...n,nf->...f/dot_general | solution.py:30
  392.4 4.3 fusion.39
  396.7 8.4 %fusion.5 = f32[64,16,512]{2,0,1:T(8,128)S(1)} fusion(f32[64,16,512]{2,1,0:T(8,128)S(1)} %select_maximum_fusion), kind=kOutput, calls=%fused_computation.18 | convolution fusion | flops 3224895488 | bytes 4194304 | tf_op jit(solution)/shard_map/...n,nf->...f/dot_general | solution.py:29
  405.1 3.6 fusion.89
  408.7 5.0 fusion.14
  413.8 4.6 convolution_add_fusion.1
  418.4 3.6 fusion.87
  422.0 3.9 convolution_negate_fusion
  426.0 4.7 fusion.11
  430.7 4.9 convolution_add_fusion
  435.6 3.8 convolution_subtract_fusion
  439.4 6.1 %multiply_subtract_fusion = (f32[128,16,512]{2,0,1:T(8,128)S(1)}, f32[128,16,512]{2,0,1:T(8,128)S(1)}) fusion(f32[128,16,512]{2,0,1:T(8,128)S(1)} %convolution_subtract_fusion, f32[128,16,512]{2,0,1:T(8,128)S(1)} %convolution_add_fusion.1, f32[128,16,512]{2,0,1:T(8,128)S(1)} %convolution_add_fusion, f32[128,16,512]{2,0,1:T(8,128)S(1)} %fusion.14, ...), kind=kOutput, calls=%fused_computation.3 | convolution fusion | flops 812761088 | bytes 27262976 | tf_op jit(solution)/shard_map/kd,d...->k.../dot_general | solution.py:52
  445.5 2.4 fusion.93
  447.9 2.8 fusion.91
  450.7 2.5 subtract_multiply_fusion
  453.2 2.5 add_multiply_fusion
  455.7 4.5 fusion.7
  460.2 4.7 fusion.29
  464.9 24.5 %all_to_all.8 = f32[64,1,16,256]{3,2,1,0:T(8,128)S(1)} all-to-all(f32[64,1,16,256]{3,2,1,0:T(8,128)S(1)} %fusion.29), channel_id=1, replica_groups=mesh['ctx'=64,'hid'=4] {'ctx'}, dimensions={0} | all-to-all | bytes 2097152 | tf_op jit(solution)/shard_map/all_to_all | solution.py:107
  489.8 7.5 %fusion = bf16[4096,256]{0,1:T(8,128)(2,1)} fusion(bf16[1024,4096]{1,0:T(8,128)(2,1)} %param.9, f32[1024,256]{0,1:T(8,128)S(1)} %copy.41, f32[1024,3,256]{0,2,1:T(8,128)} %copy-done.2), kind=kOutput, calls=%fused_computation.1 | convolution fusion | flops 2149056512 | bytes 12582912 | tf_op jit(solution)/shard_map/cd,ct->dt/dot_general | solution.py:112
  497.3 78.5 %reduce-scatter.2.cloned.1.call-done = bf16[1024,256]{0,1:T(8,128)(2,1)} async-done(((bf16[4096,256]{0,1:T(8,128)(2,1)}), bf16[1024,256]{0,1:T(8,128)(2,1)}) %reduce-scatter.2.cloned.1.call-update) | async-done | bytes 524304 | tf_op jit(solution)/shard_map/reduce_scatter | solution.py:111
  (28 shorter events, 4.0 us)
Async XLA Ops:
  6.5 320.0 %copy-start = (bf16[256,4096]{1,0:T(8,128)(2,1)S(1)}, bf16[256,4096]{1,0:T(8,128)(2,1)}, u32[]{:S(2)}) copy-start(bf16[256,4096]{1,0:T(8,128)(2,1)} %param.5) | copy-start | bytes 6291460
  6.5 320.0 %all-gather.2.cloned.1.call-start = ((), (), s32[]{:S(2)}) async-start(), calls=%async_computation.3 | async-start | bytes 25559040 | tf_op jit(solution)/shard_map/all_gather | solution.py:81
  338.3 2.1 collective-permute-start
  341.8 1.7 copy-start.2
  343.5 1.2 copy-start.6
  346.4 36.9 %all-to-all-start = ((f32[2,1,64,16,256]{4,3,1,0,2:T(8,128)}), f32[2,1,64,16,256]{4,3,1,0,2:T(8,128)S(1)}, u32[]{:S(2)}, u32[]{:S(2)}) async-start(f32[2,1,64,16,256]{4,3,1,0,2:T(8,128)} %copy.27), calls=%async_computation | async-start | bytes 4194304 | tf_op jit(solution)/shard_map/all_to_all | solution.py:97
  354.3 221.5 %reduce-scatter.2.cloned.1.call-start = ((), (), s32[]{:S(2)}) async-start(), calls=%async_computation.4 | async-start | bytes 2621440 | tf_op jit(solution)/shard_map/reduce_scatter | solution.py:111
  383.3 1.4 copy-start.3
  405.1 3.6 copy-start.5
  418.4 3.6 copy-start.4
  489.8 86.1 %copy-start.1 = (bf16[256,4096]{1,0:T(8,128)(2,1)S(1)}, bf16[256,4096]{1,0:T(8,128)(2,1)}, u32[]{:S(2)}) copy-start(bf16[256,4096]{1,0:T(8,128)(2,1)} %param.5) | copy-start | bytes 6291460
Sparse Core Ops, SparseCore 0:
  9.2 317.3 all-gather.1
  497.5 78.3 reduce-scatter.1
where the time goes:
time: 588 us; the launch traced here: 583 us
  waiting for transfers between devices  427 us (73%)
  matrix products  99 us (17%)
  blocking collectives  24.5 us (4%)
  between operations  13.9 us (2%)
  starting transfers between devices  9.4 us (2%)
  local copies, waits for them, and re-layouts  6.98 us (1%)
    all_gather x1, waiting for transfers between devices, on_device(): lax.all_gather(w_in, 'ctx', axis=1, tiled=True)  318 us
    reduce_scatter x1, waiting for transfers between devices, on_device(): lax.psum_scatter(jnp.einsum('cd,ct->dt', columns, gated, preferred_elemen...  78.5 us
    all_to_all x1, waiting for transfers between devices, on_device(): lax.all_to_all(stacked, 'ctx', split_axis=2, concat_axis=1, tiled=True)  28.8 us
    all_to_all x1, blocking collectives, on_device(): lax.all_to_all(returned, 'ctx', split_axis=0, concat_axis=1, tiled=True)  24.5 us
    dot_general x2, matrix products, spectrum_of(): real = jnp.einsum('...n,nf->...f', values, cosine, precision=HIGH)  12.6 us
    dot_general x1, matrix products, on_device(): jnp.einsum('td,jdc->cjt', columns, lax.all_gather(w_in, 'ctx', axis=1, ti...  11.8 us
  transfers between devices with their start and end apart: 4, of which 4 were waited for; matrix products, arithmetic and copies ran while one was open for 0% of the time, Pallas kernels for 0%

commit v1 on v0

v1 whole, which is shorter than its diff:
```python
import math

import numpy as np
import ml_dtypes
import jax
import jax.numpy as jnp
from jax import lax
from jax.experimental import pallas as pl
from jax.experimental.pallas import tpu as pltpu
from jax.sharding import PartitionSpec as P

MESH = pl.DeviceIdType.MESH
BF = jnp.bfloat16
F32 = jnp.float32
TAPS = 3
NY, NX, NZ = 2, 4, 8
BLK = 256
HALO = 16
ROWS = BLK + HALO
D = 4096
CQ = 256
DB = 64


def place():
    ctx = lax.axis_index("ctx")
    hid = lax.axis_index("hid")
    yl = lax.div(ctx, 32)
    x = lax.rem(lax.div(ctx, 8), 4)
    z = lax.rem(ctx, 8)
    return ctx, hid, yl, x, z


def at_ctx(yl, x, z):
    return {"ctx": yl * 32 + x * 8 + z}


class Copies:
    def __init__(self, send, recv):
        self.send, self.recv, self.all = send, recv, []

    def start(self, src, dst, device):
        k = len(self.all)
        copy = pltpu.make_async_remote_copy(
            src_ref=src,
            dst_ref=dst,
            send_sem=self.send.at[k],
            recv_sem=self.recv.at[k],
            device_id=device,
            device_id_type=MESH,
        )
        copy.start()
        self.all.append(copy)
        return copy

    def wait_sends(self):
        for copy in self.all:
            copy.wait_send()


N_COPIES = 64


def project_kernel(act, w, taps, drv, qry, abuf, wbuf, bs, local_sem, send_sem, recv_sem):
    ctx, hid, yl, x, z = place()
    core = lax.rem(hid, 2)
    mate = {"hid": hid + 1 - 2 * core}
    right, left = lax.rem(z + 1, NZ), lax.rem(z + NZ - 1, NZ)
    xr, xl, xo = lax.rem(x + 1, NX), lax.rem(x + 3, NX), lax.rem(x + 2, NX)
    after, before = lax.rem(ctx + 1, 64), lax.rem(ctx + 63, 64)
    to_r, to_l = at_ctx(yl, x, right), at_ctx(yl, x, left)
    to_y = at_ctx(1 - yl, x, z)
    to_xr, to_xl, to_xo = at_ctx(yl, xr, z), at_ctx(yl, xl, z), at_ctx(yl, xo, z)

    own_w = pltpu.make_async_copy(
        w.at[:, :, pl.ds(pl.multiple_of(x * CQ, CQ), CQ)], wbuf.at[:, yl, x, z], local_sem.at[0]
    )
    own_a = pltpu.make_async_copy(act, abuf.at[x, pl.ds(HALO, BLK)], local_sem.at[1])
    own_w.start()
    own_a.start()

    barrier = pltpu.get_barrier_semaphore()
    for peer in (to_r, to_l, to_y, to_xr, to_xl, to_xo, mate, {"ctx": after}, {"ctx": before}):
        pl.semaphore_signal(barrier, inc=1, device_id=peer, device_id_type=MESH)
    pl.semaphore_wait(barrier, 9)

    go = Copies(send_sem, recv_sem)
    first = []
    for xp, to in ((xr, to_xr), (xl, to_xl), (xo, to_xo)):
        first.append(
            go.start(w.at[:, :, pl.ds(pl.multiple_of(xp * CQ, CQ), CQ)], wbuf.at[:, yl, x, z], to)
        )
    x_next = lax.rem(lax.div(after, 8), 4)
    halo_in = go.start(act.at[pl.ds(BLK - HALO, HALO)], abuf.at[x_next, pl.ds(0, HALO)], {"ctx": after})

    def a_rows(part):
        return pl.multiple_of(core * 128 + part * 64, 64)

    def a_slot(block, part, count=64):
        return abuf.at[block, pl.ds(pl.multiple_of(HALO + core * 128 + part * 64, 16), count)]

    a_in = []
    for part, to in ((0, to_xr), (1, to_xl), (1, to_xr), (0, to_xl)):
        a_in.append(go.start(act.at[pl.ds(a_rows(part), 64)], a_slot(x, part), to))

    own_w.wait()
    for copy in first:
        copy.wait_recv()

    def piece(index, zs):
        if index == 0:
            return wbuf.at[:, yl, pl.ds(0, 2), zs]
        if index == 1:
            return wbuf.at[:, yl, pl.ds(2, 2), zs]
        if index == 2:
            return wbuf.at[:, 1 - yl, pl.ds(0, 2), zs]
        return wbuf.at[:, yl, pl.ds(index - 1, 1), zs]

    def send(index, zs, to):
        part = piece(index, zs)
        return go.start(part, part, to)

    y_in = [send(0, z, to_y)]
    from_l, from_r = {}, {}
    for index in (0, 1):
        from_l[index, 1] = send(index, z, to_r)
        from_r[index, 1] = send(index, z, to_l)
    y_in.append(send(1, z, to_y))
    y_in[0].wait_recv()
    from_l[2, 1] = send(2, z, to_r)
    from_r[2, 1] = send(2, z, to_l)

    def relay(step):
        zl, zr = lax.rem(z + NZ - step, NZ), lax.rem(z + step, NZ)
        for index in (0, 1, 2):
            from_l[index, step].wait_recv()
            if step < 3:
                from_l[index, step + 1] = send(index, zl, to_r)
            elif index == 0:
                from_l[0, 4] = send(0, zl, to_r)
            elif index == 1:
                from_l[1, 4] = send(3, zl, to_r)
            from_r[index, step].wait_recv()
            if step < 3:
                from_r[index, step + 1] = send(index, zr, to_l)
            elif index == 1:
                from_r[1, 4] = send(4, zr, to_l)
            elif index == 2:
                from_r[2, 4] = send(2, zr, to_l)
            if index == 1:
                y_in.append(send(1, zl, to_y))
                y_in.append(send(1, zr, to_y))

    relay(1)
    a_in[0].wait_recv()
    far = [go.start(a_slot(xl, 0), a_slot(xl, 0), to_xr)]
    a_in[1].wait_recv()
    far.append(go.start(a_slot(xr, 1), a_slot(xr, 1), to_xl))
    halo_in.wait_recv()
    halos = [
        go.start(abuf.at[x, pl.ds(0, HALO)], abuf.at[x, pl.ds(0, HALO)], to) for to in (to_xr, to_xl, to_xo)
    ]
    relay(2)
    a_in[2].wait_recv()
    mates = [go.start(a_slot(xl, 0, 128), a_slot(xl, 0, 128), mate)]
    a_in[3].wait_recv()
    mates.append(go.start(a_slot(xr, 0, 128), a_slot(xr, 0, 128), mate))
    relay(3)
    far[0].wait_recv()
    mates.append(go.start(a_slot(xo, 0), a_slot(xo, 0), mate))
    far[1].wait_recv()
    mates.append(go.start(a_slot(xo, 1), a_slot(xo, 1), mate))
    zo = lax.rem(z + 4, NZ)
    from_l[1, 4].wait_recv()
    y_in.append(send(3, zo, to_y))
    from_r[1, 4].wait_recv()
    y_in.append(send(4, zo, to_y))
    from_l[0, 4].wait_recv()
    from_r[2, 4].wait_recv()
    for copy in y_in[1:] + halos + mates:
        copy.wait_recv()
    own_a.wait()

    def block(xb, carry):
        keep = jnp.where(yl * 32 + xb * 8 + z == 0, 0.0, 1.0).astype(F32)
        a = abuf[xb]
        filtered = []
        for j in range(3):
            wj = wbuf[j].reshape(D, CQ)
            bs[j] = jnp.dot(a, wj, preferred_element_type=F32).astype(BF).astype(F32)
            bs[j, pl.ds(0, HALO)] = bs[j, pl.ds(0, HALO)] * keep
            total = taps[x, 3 * j][None, :] * bs[j, pl.ds(HALO, BLK)]
            for k in range(1, TAPS):
                total = total + taps[x, 3 * j + k][None, :] * bs[j, pl.ds(HALO - k, BLK)]
            filtered.append(total)
        drv[:, xb] = (filtered[0] * filtered[2]).T.astype(BF).reshape(16, 16, BLK)
        qry[xb] = filtered[1].T
        return carry

    lax.fori_loop(0, NX, block, 0)
    go.wait_sends()


def project(act, w, taps):
    return pl.pallas_call(
        project_kernel,
        out_shape=(
            jax.ShapeDtypeStruct((16, NX, 16, BLK), BF),
            jax.ShapeDtypeStruct((NX, CQ, BLK), F32),
        ),
        in_specs=[
            pl.BlockSpec(memory_space=pl.ANY),
            pl.BlockSpec(memory_space=pl.ANY),
            pl.BlockSpec(memory_space=pltpu.VMEM),
        ],
        out_specs=(pl.BlockSpec(memory_space=pltpu.VMEM), pl.BlockSpec(memory_space=pltpu.VMEM)),
        scratch_shapes=[
            pltpu.VMEM((NX, ROWS, D), BF),
            pltpu.VMEM((3, NY, NX, NZ, DB, CQ), BF),
            pltpu.VMEM((3, ROWS, CQ), F32),
            pltpu.SemaphoreType.DMA((2,)),
            pltpu.SemaphoreType.DMA((N_COPIES,)),
            pltpu.SemaphoreType.DMA((N_COPIES,)),
        ],
        compiler_params=pltpu.CompilerParams(
            collective_id=0, has_side_effects=True, vmem_limit_bytes=56 * 1024 * 1024
        ),
        name="project",
    )(act, w, taps)


def halves(table):
    high = table.astype(ml_dtypes.bfloat16)
    low = (table - high.astype(np.float64)).astype(ml_dtypes.bfloat16)
    return high, low


def tables():
    order = np.array([yl * 32 + x * 8 + z for yl in range(NY) for z in range(NZ) for x in range(NX)])
    k1 = np.arange(64) + 0.5
    angle = 2 * np.pi * np.outer(k1, np.arange(64)) / 128
    ahead = np.concatenate([np.cos(angle), -np.sin(angle)], axis=0)
    back = np.concatenate([np.cos(angle.T), -np.sin(angle.T)], axis=1) * 2.0**-14
    turn = 2 * np.pi * np.outer(k1, np.arange(BLK)) / 32768
    inner = 2 * np.pi * (np.outer(np.arange(BLK), np.arange(BLK)) % BLK) / BLK
    c, s = np.cos(inner), np.sin(inner)
    wide = np.block([[c, -s], [s, c]])
    ahead_h, ahead_l = halves(ahead[:, order])
    back_h, back_l = halves(back[order])
    wide_h, wide_l = halves(wide)
    return (
        np.concatenate([ahead_h, ahead_l], axis=1),
        np.stack([np.cos(turn), -np.sin(turn)]).astype(np.float32),
        wide_h,
        wide_l,
        np.concatenate([back_h, back_h, back_l], axis=1),
    )


GROUP = 4


def split(value):
    high = value.astype(BF)
    return high, (value - high.astype(F32)).astype(BF)


def convolve_kernel(sig, flt, ahead, turn, wide_h, wide_l, back, out, wide_sig, wide_flt, out32):
    for source, wide in ((sig, wide_sig), (flt, wide_flt)):
        for side in range(2):
            wide[side] = source[:, :, 128 * side : 128 * side + 128].astype(F32).reshape(1024, 128)

    def inner(value):
        high, low = split(value)
        return (
            jnp.dot(high, wide_h[...], preferred_element_type=F32)
            + jnp.dot(low, wide_h[...], preferred_element_type=F32)
            + jnp.dot(high, wide_l[...], preferred_element_type=F32)
        )

    def spectrum(source, first):
        parts = []
        for i in range(GROUP):
            rows = jnp.concatenate(
                [source[side, pl.ds(first + i, 64, stride=16), :] for side in range(2)], axis=1
            ).astype(BF)
            both = jnp.dot(ahead[...], jnp.concatenate([rows, rows], axis=0), preferred_element_type=F32)
            re, im = both[:64], both[64:]
            parts.append(
                jnp.concatenate([re * turn[0] - im * turn[1], re * turn[1] + im * turn[0]], axis=1)
            )
        return inner(jnp.concatenate(parts, axis=0))

    def group(g, carry):
        first = g * GROUP
        s = spectrum(wide_sig, first)
        h = spectrum(wide_flt, first)
        sr, si, hr, hi = s[:, :BLK], s[:, BLK:], h[:, :BLK], h[:, BLK:]
        product = jnp.concatenate([sr * hr - si * hi, -(sr * hi + si * hr)], axis=1)
        v = inner(product)
        for i in range(GROUP):
            re, im = v[64 * i : 64 * i + 64, :BLK], -v[64 * i : 64 * i + 64, BLK:]
            both = jnp.concatenate([re * turn[0] + im * turn[1], im * turn[0] - re * turn[1]], axis=0)
            high, low = split(both)
            y = jnp.dot(back[...], jnp.concatenate([high, low, high], axis=0), preferred_element_type=F32)
            for side in range(2):
                out32[side, pl.ds(first + i, 64, stride=16), :] = y[:, 128 * side : 128 * side + 128]
        return carry

    lax.fori_loop(0, 16 // GROUP, group, 0)
    for side in range(2):
        out[:, :, 128 * side : 128 * side + 128] = out32[side].reshape(64, 16, 128).astype(BF)


def convolve(sig, flt):
    return pl.pallas_call(
        convolve_kernel,
        out_shape=jax.ShapeDtypeStruct((64, 16, BLK), BF),
        in_specs=[pl.BlockSpec(memory_space=pltpu.VMEM)] * 7,
        out_specs=pl.BlockSpec(memory_space=pltpu.VMEM),
        scratch_shapes=[pltpu.VMEM((2, 1024, 128), F32)] * 3,
        compiler_params=pltpu.CompilerParams(vmem_limit_bytes=48 * 1024 * 1024),
        name="convolve",
    )(sig, flt, *[jnp.asarray(table) for table in tables()])


GROUPS_YZ = [[yl * 32 + x * 8 + z for yl in range(NY) for z in range(NZ)] for x in range(NX)]
GROUPS_X = [[yl * 32 + x * 8 + z for x in range(NX)] for yl in range(NY) for z in range(NZ)]


def on_device(activations, w_in, short_taps, long_filter, w_out):
    filters = long_filter.astype(BF).reshape(NX, NY * NZ, 16, BLK)
    filters = lax.all_to_all(filters, "ctx", 0, 0, axis_index_groups=GROUPS_X, tiled=True)
    filters = lax.all_to_all(filters, "ctx", 1, 1, axis_index_groups=GROUPS_YZ, tiled=True)
    filters = filters.transpose(1, 0, 2, 3).reshape(64, 16, BLK)
    taps = short_taps.transpose(0, 2, 1).reshape(9, NX, CQ).transpose(1, 0, 2)
    driven, query = project(activations, w_in, taps)
    signal = lax.all_to_all(driven, "ctx", 0, 0, axis_index_groups=GROUPS_YZ, tiled=True)
    result = convolve(signal.reshape(64, 16, BLK), filters).reshape(16, NX, 16, BLK)
    result = lax.all_to_all(result, "ctx", 0, 0, axis_index_groups=GROUPS_YZ, tiled=True)
    convolved = result.transpose(1, 0, 2, 3).reshape(NX, CQ, BLK)
    gated = (query * convolved.astype(F32)).astype(BF)
    gated = lax.all_to_all(gated, "ctx", 0, 0, axis_index_groups=GROUPS_X, tiled=True).reshape(1024, BLK)
    partial = jnp.einsum("cd,ct->dt", w_out, gated, preferred_element_type=F32).astype(BF)
    result = lax.psum_scatter(partial, "hid", scatter_dimension=0, tiled=True)
    return result.T


def solution(mesh):
    return jax.shard_map(
        on_device,
        mesh=mesh,
        in_specs=(
            P("ctx", None),
            P(None, "ctx", "hid"),
            P(None, "hid", None),
            P("hid", "ctx"),
            P("hid", None),
        ),
        out_specs=P("ctx", "hid"),
        check_vma=False,
    )
```

time: 588 us -> 225 us (0.38)
  waiting for transfers between devices: 427 us -> 56.8 us
  matrix products: 99 us -> 7.09 us
  Pallas kernels: 0 us -> 84.3 us
  blocking collectives: 24.5 us -> 50.2 us
    all_gather x1 -> x0, waiting for transfers between devices: 318 us -> none  [on_device(): lax.all_gather(w_in, 'ctx', axis=1, tiled=True)]
    dot_general x20 -> x1, matrix products: 99 us -> 7.09 us  [on_device(): jnp.einsum('cd,ct->dt', w_out, gated, preferred_element_type=F32).astype(BF)]
    pallas_call x0 -> x2, Pallas kernels: none -> 84.3 us  [the longest x1 75.5 us: project(): pl.pallas_call(project_kernel, out_shape=(jax.ShapeDtypeStruct((16, NX, 1...]
    reduce_scatter x1, waiting for transfers between devices: 78.5 us -> 44.7 us  [on_device(): result = lax.psum_scatter(partial, 'hid', scatter_dimension=0, tiled=True)]
    all_to_all x1 -> x3, blocking collectives: 24.5 us -> 50.2 us  [the longest x1 19.4 us: on_device(): lax.all_to_all(result, 'ctx', 0, 0, axis_index_groups=GROUPS_YZ, tiled=True)]
    all_to_all x1 -> x2, waiting for transfers between devices: 28.8 us -> 12.1 us  [the longest x1 12.1 us: on_device(): lax.all_to_all(driven, 'ctx', 0, 0, axis_index_groups=GROUPS_YZ, tiled=True)]
  transfers between devices with their start and end apart: 4 -> 3, of which waited for: 4 -> 2; matrix products, arithmetic and copies ran while one was open for 0% -> 1% of each run, Pallas kernels for 0% -> 34%
where the time goes in v1:
time: 225 us; the launch traced here: 224 us
  Pallas kernels  84.3 us (37%)
  waiting for transfers between devices  56.8 us (25%)
  blocking collectives  50.2 us (22%)
  between operations  13.5 us (6%)
  starting transfers between devices  8.47 us (4%)
  matrix products  7.09 us (3%)
  other arithmetic  2.44 us (1%)
    pallas_call x1, Pallas kernels, project(): pl.pallas_call(project_kernel, out_shape=(jax.ShapeDtypeStruct((16, NX, 1...  75.5 us
    reduce_scatter x1, waiting for transfers between devices, on_device(): result = lax.psum_scatter(partial, 'hid', scatter_dimension=0, tiled=True)  44.7 us
    all_to_all x1, blocking collectives, on_device(): lax.all_to_all(result, 'ctx', 0, 0, axis_index_groups=GROUPS_YZ, tiled=True)  19.4 us
    all_to_all x1, blocking collectives, on_device(): lax.all_to_all(filters, 'ctx', 1, 1, axis_index_groups=GROUPS_YZ, tiled=T...  18.8 us
    all_to_all x1, waiting for transfers between devices, on_device(): lax.all_to_all(driven, 'ctx', 0, 0, axis_index_groups=GROUPS_YZ, tiled=True)  12.1 us
    all_to_all x1, blocking collectives, on_device(): lax.all_to_all(gated, 'ctx', 0, 0, axis_index_groups=GROUPS_X, tiled=True)  12.1 us
    pallas_call x1, Pallas kernels, convolve(): pl.pallas_call(convolve_kernel, out_shape=jax.ShapeDtypeStruct((64, 16, B...  8.79 us
    dot_general x1, matrix products, on_device(): jnp.einsum('cd,ct->dt', w_out, gated, preferred_element_type=F32).astype(BF)  7.09 us
  transfers between devices with their start and end apart: 3, of which 2 were waited for; matrix products, arithmetic and copies ran while one was open for 1% of the time, Pallas kernels for 34%

profile of v1, /device:TPU:1, one launch (start us, length us, event | category | flops | bytes accessed | tf_op | source)
XLA Modules:
  0.0 224.4 jit_solution(15948094555215719414)
XLA Ops:
  6.5 0.0 copy-start.3
  6.5 0.0 copy-start
  6.5 0.0 copy-start.1
  6.5 0.0 copy-start.2
  6.5 0.0 copy-start.4
  6.6 2.2 convert_element_type.21
  8.7 4.8 %all-to-all-start.1 = ((bf16[4,16,16,256]{3,2,1,0:T(8,128)(2,1)}), bf16[4,16,16,256]{3,2,1,0:T(8,128)(2,1)S(1)}, u32[]{:S(2)}, u32[]{:S(2)}) async-start(bf16[4,16,16,256]{3,2,1,0:T(8,128)(2,1)} %bitcast.3), calls=%async_computation.1 | async-start | bytes 1048576 | tf_op jit(solution)/shard_map/all_to_all | solution.py:333
  13.6 0.8 reshape.21
  14.4 0.6 copy.23
  15.0 75.5 %project.1 = (bf16[16,4,16,256]{3,2,1,0:T(8,128)(2,1)}, f32[4,256,256]{2,1,0:T(8,128)}) custom-call(bf16[256,4096]{1,0:T(8,128)(2,1)} %act.1, bf16[3,64,1024]{2,1,0:T(8,128)(2,1)} %w.1, f32[4,9,256]{2,1,0:T(8,128)} %bitcast.26), custom_call_target="tpu_custom_call" | custom-call | tf_op jit(solution)/shard_map/project/pallas_call | solution.py:205
  90.5 0.0 all-to-all-done.1
  90.5 3.6 %all-to-all-start = ((bf16[16,4,16,256]{3,2,1,0:T(8,128)(2,1)}), bf16[16,4,16,256]{3,2,1,0:T(8,128)(2,1)S(1)}, u32[]{:S(2)}, u32[]{:S(2)}) async-start(bf16[16,4,16,256]{3,2,1,0:T(8,128)(2,1)} %get-tuple-element.8), calls=%async_computation | async-start | bytes 1048576 | tf_op jit(solution)/shard_map/all_to_all | solution.py:338
  94.1 0.0 reduce-scatter.2.cloned.1.call-start
  94.2 12.1 %all-to-all-done = bf16[16,4,16,256]{3,2,1,0:T(8,128)(2,1)S(1)} async-done(((bf16[16,4,16,256]{3,2,1,0:T(8,128)(2,1)}), bf16[16,4,16,256]{3,2,1,0:T(8,128)(2,1)S(1)}, u32[]{:S(2)}, u32[]{:S(2)}) %all-to-all-start) | async-done | bytes 524320 | tf_op jit(solution)/shard_map/all_to_all | solution.py:338
  106.3 0.0 copy-start.5
  106.3 18.8 %all_to_all.25 = bf16[4,16,16,256]{3,2,0,1:T(8,128)(2,1)S(1)} all-to-all(bf16[4,16,16,256]{3,2,0,1:T(8,128)(2,1)S(1)} %copy.20), channel_id=1, replica_groups={{0,4,8,12,16,20,24,28,128,132,136,140,144,148,152,156},{32,36,40,44,48,..., dimensions={1} | all-to-all | bytes 1048576 | tf_op jit(solution)/shard_map/all_to_all | solution.py:334
  125.1 0.0 copy-done.3
  125.1 0.0 copy-done
  125.1 0.0 copy-done.1
  125.1 0.0 copy-done.2
  125.1 0.0 copy-done.4
  125.1 8.8 %convolve.1 = bf16[64,16,256]{2,1,0:T(8,128)(2,1)S(1)} custom-call(bf16[64,16,256]{2,1,0:T(8,128)(2,1)S(1)} %bitcast.22, bf16[64,16,256]{2,1,0:T(8,128)(2,1)S(1)} %bitcast.23, bf16[128,128]{1,0:T(8,128)(2,1)S(1)} %copy-done.4, f32[2,64,256]{2,1,0:T(8,128)S(1)} %copy-done.2, bf16[512,512]{1,0:T(8,128)(2,1)S(1)} %copy-done.1, bf16[512,512]{1,0:T(8,128)(2,1)S(1)} %copy-done, ...), custom_call_target="tpu_custom_call" | custom-call | tf_op jit(solution)/shard_map/convolve/pallas_call | solution.py:316
  133.9 19.4 %all_to_all.26 = bf16[16,4,16,256]{3,2,1,0:T(8,128)(2,1)S(1)} all-to-all(bf16[16,4,16,256]{3,2,1,0:T(8,128)(2,1)S(1)} %bitcast.24), channel_id=1, replica_groups={{0,4,8,12,16,20,24,28,128,132,136,140,144,148,152,156},{32,36,40,44,48,..., dimensions={0} | all-to-all | bytes 1048576 | tf_op jit(solution)/shard_map/all_to_all | solution.py:340
  153.3 0.1 convert_bitcast_fusion
  153.4 0.1 copy.21
  153.5 0.0 copy-done.5
  153.6 0.1 fusion.1
  153.7 12.1 %all_to_all.27 = bf16[4,256,256]{2,1,0:T(8,128)(2,1)S(1)} all-to-all(bf16[4,256,256]{2,1,0:T(8,128)(2,1)S(1)} %fusion.1), channel_id=1, replica_groups={{0,32,64,96},{4,36,68,100},{8,40,72,104},{12,44,76,108},{16,48,80,112},..., dimensions={0} | all-to-all | bytes 1048576 | tf_op jit(solution)/shard_map/all_to_all | solution.py:343
  165.8 7.1 %fusion = bf16[4096,256]{0,1:T(8,128)(2,1)} fusion(bf16[1024,256]{1,0:T(8,128)(2,1)S(1)} %bitcast.25, bf16[1024,4096]{1,0:T(8,128)(2,1)} %param.14), kind=kOutput, calls=%fused_computation.1 | convolution fusion | flops 2148532224 | bytes 11010048 | tf_op jit(solution)/shard_map/cd,ct->dt/dot_general | solution.py:344
  172.8 0.0 reduce-scatter.2.cloned.1.call-update
  172.9 44.7 %reduce-scatter.2.cloned.1.call-done = bf16[1024,256]{0,1:T(8,128)(2,1)} async-done(((bf16[4096,256]{0,1:T(8,128)(2,1)}), bf16[1024,256]{0,1:T(8,128)(2,1)}) %reduce-scatter.2.cloned.1.call-update) | async-done | bytes 524304 | tf_op jit(solution)/shard_map/reduce_scatter | solution.py:345
  (1 shorter events, 0.0 us)
Async XLA Ops:
  6.5 118.6 %copy-start.3 = (bf16[64,384]{1,0:T(8,128)(2,1)S(1)}, bf16[64,384]{1,0:T(8,128)(2,1)}, u32[]{:S(2)}) copy-start(bf16[64,384]{1,0:T(8,128)(2,1)} %constant.14.clone.back) | copy-start | bytes 147460
  6.5 118.6 %copy-start = (bf16[512,512]{1,0:T(8,128)(2,1)S(1)}, bf16[512,512]{1,0:T(8,128)(2,1)}, u32[]{:S(2)}) copy-start(bf16[512,512]{1,0:T(8,128)(2,1)} %constant.13.clone.wide_l) | copy-start | bytes 1572868
  6.5 118.6 %copy-start.1 = (bf16[512,512]{1,0:T(8,128)(2,1)S(1)}, bf16[512,512]{1,0:T(8,128)(2,1)}, u32[]{:S(2)}) copy-start(bf16[512,512]{1,0:T(8,128)(2,1)} %constant.12.clone.wide_h) | copy-start | bytes 1572868
  6.5 118.6 %copy-start.2 = (f32[2,64,256]{2,1,0:T(8,128)S(1)}, f32[2,64,256]{2,1,0:T(8,128)}, u32[]{:S(2)}) copy-start(f32[2,64,256]{2,1,0:T(8,128)} %constant.11.clone.turn) | copy-start | bytes 393220
  6.5 118.6 %copy-start.4 = (bf16[128,128]{1,0:T(8,128)(2,1)S(1)}, bf16[128,128]{1,0:T(8,128)(2,1)}, u32[]{:S(2)}) copy-start(bf16[128,128]{1,0:T(8,128)(2,1)} %constant.10.clone.ahead) | copy-start | bytes 98308
  8.7 81.8 %all-to-all-start.1 = ((bf16[4,16,16,256]{3,2,1,0:T(8,128)(2,1)}), bf16[4,16,16,256]{3,2,1,0:T(8,128)(2,1)S(1)}, u32[]{:S(2)}, u32[]{:S(2)}) async-start(bf16[4,16,16,256]{3,2,1,0:T(8,128)(2,1)} %bitcast.3), calls=%async_computation.1 | async-start | bytes 1048576 | tf_op jit(solution)/shard_map/all_to_all | solution.py:333
  90.5 15.8 %all-to-all-start = ((bf16[16,4,16,256]{3,2,1,0:T(8,128)(2,1)}), bf16[16,4,16,256]{3,2,1,0:T(8,128)(2,1)S(1)}, u32[]{:S(2)}, u32[]{:S(2)}) async-start(bf16[16,4,16,256]{3,2,1,0:T(8,128)(2,1)} %get-tuple-element.8), calls=%async_computation | async-start | bytes 1048576 | tf_op jit(solution)/shard_map/all_to_all | solution.py:338
  94.1 123.5 %reduce-scatter.2.cloned.1.call-start = ((), (), s32[]{:S(2)}) async-start(), calls=%async_computation.6 | async-start | bytes 2621440 | tf_op jit(solution)/shard_map/reduce_scatter | solution.py:345
  106.3 47.3 %copy-start.5 = (f32[4,256,256]{2,1,0:T(8,128)S(1)}, f32[4,256,256]{2,1,0:T(8,128)}, u32[]{:S(2)}) copy-start(f32[4,256,256]{2,1,0:T(8,128)} %get-tuple-element.7) | copy-start | bytes 3145732
Sparse Core Ops, SparseCore 0:
  173.0 44.5 reduce-scatter.1

commit v2 on v1

v2 whole, which is shorter than its diff:
```python
import math

import numpy as np
import ml_dtypes
import jax
import jax.numpy as jnp
from jax import lax
from jax.experimental import pallas as pl
from jax.experimental.pallas import tpu as pltpu
from jax.sharding import PartitionSpec as P

MESH = pl.DeviceIdType.MESH
BF = jnp.bfloat16
F32 = jnp.float32
TAPS = 3
NY, NX, NZ = 2, 4, 8
BLK = 256
HALO = 16
ROWS = BLK + HALO
D = 4096
CQ = 256
DB = 64


def place():
    ctx = lax.axis_index("ctx")
    hid = lax.axis_index("hid")
    yl = lax.div(ctx, 32)
    x = lax.rem(lax.div(ctx, 8), 4)
    z = lax.rem(ctx, 8)
    return ctx, hid, yl, x, z


def at_ctx(yl, x, z):
    return {"ctx": yl * 32 + x * 8 + z}


class Copies:
    def __init__(self, send, recv):
        self.send, self.recv, self.all = send, recv, []

    def start(self, src, dst, device):
        k = len(self.all)
        copy = pltpu.make_async_remote_copy(
            src_ref=src,
            dst_ref=dst,
            send_sem=self.send.at[k],
            recv_sem=self.recv.at[k],
            device_id=device,
            device_id_type=MESH,
        )
        copy.start()
        self.all.append(copy)
        return copy

    def wait_sends(self):
        for copy in self.all:
            copy.wait_send()


def halves(table):
    high = table.astype(ml_dtypes.bfloat16)
    low = (table - high.astype(np.float64)).astype(ml_dtypes.bfloat16)
    return high, low


def tables():
    order = np.array([yl * 32 + x * 8 + z for yl in range(NY) for z in range(NZ) for x in range(NX)])
    k1 = np.arange(64) + 0.5
    angle = 2 * np.pi * np.outer(k1, np.arange(64)) / 128
    ahead = np.concatenate([np.cos(angle), -np.sin(angle)], axis=0)
    back = np.concatenate([np.cos(angle.T), -np.sin(angle.T)], axis=1) * 2.0**-14
    turn = 2 * np.pi * np.outer(k1, np.arange(BLK)) / 32768
    inner = 2 * np.pi * (np.outer(np.arange(BLK), np.arange(BLK)) % BLK) / BLK
    c, s = np.cos(inner), np.sin(inner)
    wide = np.block([[c, -s], [s, c]])
    ahead_h, ahead_l = halves(ahead[:, order])
    back_h, back_l = halves(back[order])
    wide_h, wide_l = halves(wide)
    return (
        np.concatenate([ahead_h, ahead_l], axis=1),
        np.stack([np.cos(turn), -np.sin(turn)]).astype(np.float32),
        wide_h,
        wide_l,
        np.concatenate([back_h, back_h, back_l], axis=1),
    )


N_COPIES = 64
GROUP = 4


def split(value):
    high = value.astype(BF)
    return high, (value - high.astype(F32)).astype(BF)


def layer_kernel(
    act, w, taps, flt, w_out, ahead, turn, wide_h, wide_l, back, out,
    abuf, wbuf, bs, f32buf, f16buf, fx, frecv, drv, drecv, qry, qrecv, wide, out32, spec, osend, crecv,
    obuf, psend, precv, ysend, yrecv, local_sem, own_sem, all_send, all_recv, send_sem, recv_sem,
):
    ctx, hid, yl, x, z = place()
    core = lax.rem(hid, 2)
    yh = lax.div(hid, 2)
    mate = {"hid": hid + 1 - 2 * core}
    across = {"hid": lax.rem(hid + 2, 4)}
    me = yl * NZ + z
    right, left = lax.rem(z + 1, NZ), lax.rem(z + NZ - 1, NZ)
    xr, xl, xo = lax.rem(x + 1, NX), lax.rem(x + 3, NX), lax.rem(x + 2, NX)
    after = lax.rem(ctx + 1, 64)
    to_r, to_l = at_ctx(yl, x, right), at_ctx(yl, x, left)
    to_y = at_ctx(1 - yl, x, z)
    to_xr, to_xl, to_xo = at_ctx(yl, xr, z), at_ctx(yl, xl, z), at_ctx(yl, xo, z)

    own_w = pltpu.make_async_copy(
        w.at[:, :, pl.ds(pl.multiple_of(x * CQ, CQ), CQ)], wbuf.at[:, yl, x, z], local_sem.at[0]
    )
    own_a = pltpu.make_async_copy(act, abuf.at[x, pl.ds(HALO, BLK)], local_sem.at[1])
    own_w.start()
    own_a.start()

    own_f = pltpu.make_async_copy(flt, f32buf, local_sem.at[2])
    own_f.start()
    own_o = [
        pltpu.make_async_copy(w_out.at[:, pl.ds(1024 * h, 1024)], obuf.at[h], local_sem.at[3 + h])
        for h in range(4)
    ]
    for copy in own_o:
        copy.start()

    barrier = pltpu.get_barrier_semaphore()

    def greet(t, carry):
        pl.semaphore_signal(barrier, inc=1, device_id={"ctx": lax.rem(ctx + t, 64)}, device_id_type=MESH)
        return carry

    lax.fori_loop(1, 64, greet, 0)
    for peer in (mate, across):
        pl.semaphore_signal(barrier, inc=1, device_id=peer, device_id_type=MESH)
    pl.semaphore_wait(barrier, 65)

    go = Copies(send_sem, recv_sem)

    def spread(src, dst, sem):
        def one(t, carry):
            p = lax.rem(me + t, 16)
            pltpu.make_async_remote_copy(
                src_ref=src(p),
                dst_ref=dst,
                send_sem=all_send.at[sem],
                recv_sem=all_recv.at[sem],
                device_id=at_ctx(lax.div(p, NZ), x, lax.rem(p, NZ)),
                device_id_type=MESH,
            ).start()
            return carry

        lax.fori_loop(1, 16, one, 0)

    def to_all(src, dst, sem):
        spread(lambda p: src.at[p], dst.at[me], sem)
        pltpu.make_async_copy(src.at[me], dst.at[me], own_sem.at[sem]).start()

    def await_all(src, dst, sem):
        pltpu.make_async_copy(src.at[me], dst.at[me], own_sem.at[sem]).wait()
        pltpu.make_async_copy(dst.at[pl.ds(0, 15)], dst.at[pl.ds(0, 15)], all_recv.at[sem]).wait()

    def sent_all(src, sem, count=15):
        pltpu.make_async_copy(src.at[pl.ds(0, count)], src.at[pl.ds(0, count)], all_send.at[sem]).wait()

    first = []
    for xp, to in ((xr, to_xr), (xl, to_xl), (xo, to_xo)):
        first.append(
            go.start(w.at[:, :, pl.ds(pl.multiple_of(xp * CQ, CQ), CQ)], wbuf.at[:, yl, x, z], to)
        )
    x_next = lax.rem(lax.div(after, 8), 4)
    halo_in = go.start(act.at[pl.ds(BLK - HALO, HALO)], abuf.at[x_next, pl.ds(0, HALO)], {"ctx": after})

    def a_rows(part):
        return pl.multiple_of(core * 128 + part * 64, 64)

    def a_slot(block, part, count=64):
        return abuf.at[block, pl.ds(pl.multiple_of(HALO + core * 128 + part * 64, 16), count)]

    a_in = []
    for part, to in ((0, to_xr), (1, to_xl), (1, to_xr), (0, to_xl)):
        a_in.append(go.start(act.at[pl.ds(a_rows(part), 64)], a_slot(x, part), to))

    own_f.wait()
    f16buf[...] = f32buf[...].astype(BF).reshape(NX, 16, 16, BLK)
    own_x = pltpu.make_async_copy(f16buf.at[x], fx.at[:, x], local_sem.at[2])
    own_x.start()
    fx_in = [go.start(f16buf.at[xp], fx.at[:, x], to) for xp, to in ((xr, to_xr), (xl, to_xl), (xo, to_xo))]

    own_w.wait()
    for copy in first:
        copy.wait_recv()

    def piece(index, zs):
        if index == 0:
            return wbuf.at[:, yl, pl.ds(0, 2), zs]
        if index == 1:
            return wbuf.at[:, yl, pl.ds(2, 2), zs]
        if index == 2:
            return wbuf.at[:, 1 - yl, pl.ds(0, 2), zs]
        return wbuf.at[:, yl, pl.ds(index - 1, 1), zs]

    def send(index, zs, to):
        part = piece(index, zs)
        return go.start(part, part, to)

    y_in = [send(0, z, to_y)]
    from_l, from_r = {}, {}
    for index in (0, 1):
        from_l[index, 1] = send(index, z, to_r)
        from_r[index, 1] = send(index, z, to_l)
    y_in.append(send(1, z, to_y))
    y_in[0].wait_recv()
    from_l[2, 1] = send(2, z, to_r)
    from_r[2, 1] = send(2, z, to_l)

    def relay(step):
        zl, zr = lax.rem(z + NZ - step, NZ), lax.rem(z + step, NZ)
        for index in (0, 1, 2):
            from_l[index, step].wait_recv()
            if step < 3:
                from_l[index, step + 1] = send(index, zl, to_r)
            elif index == 0:
                from_l[0, 4] = send(0, zl, to_r)
            elif index == 1:
                from_l[1, 4] = send(3, zl, to_r)
            from_r[index, step].wait_recv()
            if step < 3:
                from_r[index, step + 1] = send(index, zr, to_l)
            elif index == 1:
                from_r[1, 4] = send(4, zr, to_l)
            elif index == 2:
                from_r[2, 4] = send(2, zr, to_l)
            if index == 1:
                y_in.append(send(1, zl, to_y))
                y_in.append(send(1, zr, to_y))

    relay(1)
    a_in[0].wait_recv()
    far = [go.start(a_slot(xl, 0), a_slot(xl, 0), to_xr)]
    a_in[1].wait_recv()
    far.append(go.start(a_slot(xr, 1), a_slot(xr, 1), to_xl))
    halo_in.wait_recv()
    halos = [
        go.start(abuf.at[x, pl.ds(0, HALO)], abuf.at[x, pl.ds(0, HALO)], to) for to in (to_xr, to_xl, to_xo)
    ]
    relay(2)
    a_in[2].wait_recv()
    mates = [go.start(a_slot(xl, 0, 128), a_slot(xl, 0, 128), mate)]
    a_in[3].wait_recv()
    mates.append(go.start(a_slot(xr, 0, 128), a_slot(xr, 0, 128), mate))
    relay(3)
    far[0].wait_recv()
    mates.append(go.start(a_slot(xo, 0), a_slot(xo, 0), mate))
    far[1].wait_recv()
    mates.append(go.start(a_slot(xo, 1), a_slot(xo, 1), mate))
    zo = lax.rem(z + 4, NZ)
    from_l[1, 4].wait_recv()
    y_in.append(send(3, zo, to_y))
    from_r[1, 4].wait_recv()
    y_in.append(send(4, zo, to_y))
    from_l[0, 4].wait_recv()
    from_r[2, 4].wait_recv()
    own_x.wait()
    for copy in fx_in:
        copy.wait_recv()
    to_all(fx, frecv, 1)
    for copy in y_in[1:] + halos + mates:
        copy.wait_recv()
    own_a.wait()


    def block(xb, carry):
        keep = jnp.where(yl * 32 + xb * 8 + z == 0, 0.0, 1.0).astype(F32)
        a = abuf[xb]
        filtered = []
        for j in range(3):
            wj = wbuf[j].reshape(D, CQ)
            bs[j] = jnp.dot(a, wj, preferred_element_type=F32).astype(BF).astype(F32)
            bs[j, pl.ds(0, HALO)] = bs[j, pl.ds(0, HALO)] * keep
            lanes = pl.ds(pl.multiple_of(x * CQ, CQ), CQ)
            total = taps[j, pl.ds(0, 1), lanes] * bs[j, pl.ds(HALO, BLK)]
            for k in range(1, TAPS):
                total = total + taps[j, pl.ds(k, 1), lanes] * bs[j, pl.ds(HALO - k, BLK)]
            filtered.append(total)
        drv[:, xb] = (filtered[0] * filtered[2]).T.astype(BF).reshape(16, 16, BLK)
        spread(lambda p: drv.at[p, xb], drecv.at[me, xb], 0)
        qry[xb] = filtered[1].T.astype(BF)
        return carry

    lax.fori_loop(0, NX, block, 0)
    pltpu.make_async_copy(drv.at[me], drecv.at[me], own_sem.at[0]).start()
    own_q = pltpu.make_async_copy(qry.at[x], qrecv.at[x], local_sem.at[0])
    own_q.start()
    q_in = [go.start(qry.at[xp], qrecv.at[x], to) for xp, to in ((xr, to_xr), (xl, to_xl), (xo, to_xo))]

    def inner(value):
        high, low = split(value)
        return (
            jnp.dot(high, wide_h[...], preferred_element_type=F32)
            + jnp.dot(low, wide_h[...], preferred_element_type=F32)
            + jnp.dot(high, wide_l[...], preferred_element_type=F32)
        )

    def widen(source):
        for side in range(2):
            half = source[:, :, :, 128 * side : 128 * side + 128]
            wide[side] = half.astype(F32).reshape(1024, 128)

    def spectrum(first):
        parts = []
        for i in range(GROUP):
            rows = jnp.concatenate(
                [wide[side, pl.ds(first + i, 64, stride=16), :] for side in range(2)], axis=1
            ).astype(BF)
            both = jnp.dot(ahead[...], jnp.concatenate([rows, rows], axis=0), preferred_element_type=F32)
            re, im = both[:64], both[64:]
            parts.append(
                jnp.concatenate([re * turn[0] - im * turn[1], re * turn[1] + im * turn[0]], axis=1)
            )
        return inner(jnp.concatenate(parts, axis=0))

    def filter_group(g, carry):
        spec[g] = spectrum(g * GROUP)
        return carry

    def signal_group(g, carry):
        first = g * GROUP
        s = spectrum(first)
        sr, si, hr, hi = s[:, :BLK], s[:, BLK:], spec[g, :, :BLK], spec[g, :, BLK:]
        v = inner(jnp.concatenate([sr * hr - si * hi, -(sr * hi + si * hr)], axis=1))
        for i in range(GROUP):
            re, im = v[64 * i : 64 * i + 64, :BLK], -v[64 * i : 64 * i + 64, BLK:]
            both = jnp.concatenate([re * turn[0] + im * turn[1], im * turn[0] - re * turn[1]], axis=0)
            high, low = split(both)
            y = jnp.dot(back[...], jnp.concatenate([high, low, high], axis=0), preferred_element_type=F32)
            for side in range(2):
                out32[side, pl.ds(first + i, 64, stride=16), :] = y[:, 128 * side : 128 * side + 128]
        return carry

    await_all(fx, frecv, 1)
    widen(frecv)
    lax.fori_loop(0, 16 // GROUP, filter_group, 0)
    await_all(drv, drecv, 0)
    widen(drecv)
    lax.fori_loop(0, 16 // GROUP, signal_group, 0)
    for side in range(2):
        osend[:, :, 128 * side : 128 * side + 128] = out32[side].reshape(64, 16, 128).astype(BF)

    slot = x * 16 + me

    def home(t, carry):
        c = lax.rem(ctx + t, 64)
        yt, xt, zt = lax.div(c, 32), lax.rem(lax.div(c, 8), 4), lax.rem(c, 8)
        pltpu.make_async_remote_copy(
            src_ref=osend.at[(yt * NZ + zt) * NX + xt],
            dst_ref=crecv.at[slot],
            send_sem=all_send.at[2],
            recv_sem=all_recv.at[2],
            device_id={"ctx": c},
            device_id_type=MESH,
        ).start()
        return carry

    lax.fori_loop(1, 64, home, 0)
    own_c = pltpu.make_async_copy(osend.at[me * NX + x], crecv.at[slot], own_sem.at[2])
    own_c.start()
    own_q.wait()
    for copy in q_in:
        copy.wait_recv()
    for copy in own_o:
        copy.wait()
    own_c.wait()
    pltpu.make_async_copy(crecv.at[pl.ds(0, 63)], crecv.at[pl.ds(0, 63)], all_recv.at[2]).wait()
    gated = (qrecv[...].reshape(1024, BLK).astype(F32) * crecv[...].reshape(1024, BLK).astype(F32)).astype(BF)
    gated = gated.T

    def partial(h):
        return jnp.dot(gated, obuf[h], preferred_element_type=F32)

    far_h, near_h = (1 - yh) * 2, yh * 2
    psend[0] = partial(far_h + 1 - core).astype(BF)
    p_in = [go.start(psend.at[0], precv.at[0], mate)]
    total = partial(far_h + core)
    p_in[0].wait_recv()
    ysend[...] = (total + precv[0].astype(F32)).astype(BF)
    y_copy = go.start(ysend, yrecv, across)
    psend[1] = partial(near_h + 1 - core).astype(BF)
    p_in.append(go.start(psend.at[1], precv.at[1], mate))
    total = partial(near_h + core)
    p_in[1].wait_recv()
    total = total + precv[1].astype(F32)
    y_copy.wait_recv()
    out[...] = (total + yrecv[...].astype(F32)).astype(BF)

    go.wait_sends()
    sent_all(drv, 0)
    sent_all(fx, 1)
    sent_all(osend, 2, 63)


def layer(act, w, taps, flt, w_out):
    any_space, vmem = pl.BlockSpec(memory_space=pl.ANY), pl.BlockSpec(memory_space=pltpu.VMEM)
    return pl.pallas_call(
        layer_kernel,
        out_shape=jax.ShapeDtypeStruct((BLK, 1024), BF),
        in_specs=[any_space, any_space, vmem, any_space, any_space] + [vmem] * 5,
        out_specs=vmem,
        scratch_shapes=[
            pltpu.VMEM((NX, ROWS, D), BF),
            pltpu.VMEM((3, NY, NX, NZ, DB, CQ), BF),
            pltpu.VMEM((3, ROWS, CQ), F32),
            pltpu.VMEM((1024, BLK), F32),
            pltpu.VMEM((NX, 16, 16, BLK), BF),
            pltpu.VMEM((16, NX, 16, BLK), BF),
            pltpu.VMEM((16, NX, 16, BLK), BF),
            pltpu.VMEM((16, NX, 16, BLK), BF),
            pltpu.VMEM((16, NX, 16, BLK), BF),
            pltpu.VMEM((NX, CQ, BLK), BF),
            pltpu.VMEM((NX, CQ, BLK), BF),
            pltpu.VMEM((2, 1024, 128), F32),
            pltpu.VMEM((2, 1024, 128), F32),
            pltpu.VMEM((16 // GROUP, 64 * GROUP, 2 * BLK), F32),
            pltpu.VMEM((64, 16, BLK), BF),
            pltpu.VMEM((64, 16, BLK), BF),
            pltpu.VMEM((4, 1024, 1024), BF),
            pltpu.VMEM((2, BLK, 1024), BF),
            pltpu.VMEM((2, BLK, 1024), BF),
            pltpu.VMEM((BLK, 1024), BF),
            pltpu.VMEM((BLK, 1024), BF),
            pltpu.SemaphoreType.DMA((8,)),
            pltpu.SemaphoreType.DMA((3,)),
            pltpu.SemaphoreType.DMA((3,)),
            pltpu.SemaphoreType.DMA((3,)),
            pltpu.SemaphoreType.DMA((N_COPIES,)),
            pltpu.SemaphoreType.DMA((N_COPIES,)),
        ],
        compiler_params=pltpu.CompilerParams(
            collective_id=0, has_side_effects=True, vmem_limit_bytes=58 * 1024 * 1024
        ),
        name="layer",
    )(act, w, taps, flt, w_out, *[jnp.asarray(table) for table in tables()])


def on_device(activations, w_in, short_taps, long_filter, w_out):
    return layer(activations, w_in, short_taps.transpose(0, 2, 1), long_filter, w_out)


def solution(mesh):
    return jax.shard_map(
        on_device,
        mesh=mesh,
        in_specs=(
            P("ctx", None),
            P(None, "ctx", "hid"),
            P(None, "hid", None),
            P("hid", "ctx"),
            P("hid", None),
        ),
        out_specs=P("ctx", "hid"),
        check_vma=False,
    )
```

time: 225 us -> 135 us (0.60)
  waiting for transfers between devices: 56.8 us -> 0 us
  blocking collectives: 50.2 us -> 0 us
  Pallas kernels: 84.3 us -> 133 us
  between operations: 13.5 us -> 0.01 us
  starting transfers between devices: 8.47 us -> 0 us
  matrix products: 7.09 us -> 0 us
  other arithmetic: 2.44 us -> 0 us
    all_to_all x3 -> x0, blocking collectives: 50.2 us -> none  [the longest x1 19.4 us: on_device(): lax.all_to_all(result, 'ctx', 0, 0, axis_index_groups=GROUPS_YZ, tiled=True)]
    pallas_call x2 -> x1, Pallas kernels: 84.3 us -> 133 us  [layer(): pl.pallas_call(layer_kernel, out_shape=jax.ShapeDtypeStruct((BLK, 1024),...]
    reduce_scatter x1 -> x0, waiting for transfers between devices: 44.7 us -> none  [on_device(): result = lax.psum_scatter(partial, 'hid', scatter_dimension=0, tiled=True)]
    all_to_all x2 -> x0, waiting for transfers between devices: 12.1 us -> none  [the longest x1 12.1 us: on_device(): lax.all_to_all(driven, 'ctx', 0, 0, axis_index_groups=GROUPS_YZ, tiled=True)]
    all_to_all x2 -> x0, starting transfers between devices: 8.43 us -> none  [the longest x1 4.84 us: on_device(): lax.all_to_all(filters, 'ctx', 0, 0, axis_index_groups=GROUPS_X, tiled=True)]
    dot_general x1 -> x0, matrix products: 7.09 us -> none  [on_device(): jnp.einsum('cd,ct->dt', w_out, gated, preferred_element_type=F32).astype(BF)]
    convert_element_type x3 -> x0, other arithmetic: 2.44 us -> none  [the longest x1 2.17 us: on_device(): filters = long_filter.astype(BF).reshape(NX, NY * NZ, 16, BLK)]
  transfers between devices with their start and end apart: 3 -> 0, of which waited for: 2 -> 0; matrix products, arithmetic and copies ran while one was open for 1% -> 0% of each run, Pallas kernels for 34% -> 0%
where the time goes in v2:
time: 135 us
  Pallas kernels  133 us (99%)
  local copies, waits for them, and re-layouts  1.87 us (1%)
    pallas_call x1, Pallas kernels, layer(): pl.pallas_call(layer_kernel, out_shape=jax.ShapeDtypeStruct((BLK, 1024),...  133 us

profile of v2, /device:TPU:1, one launch (start us, length us, event | category | flops | bytes accessed | tf_op | source)
XLA Modules:
  0.0 135.2 jit_solution(4940984682650532951)
XLA Ops:
  0.0 133.3 %layer.1 = bf16[256,1024]{1,0:T(8,128)(2,1)} custom-call(bf16[256,4096]{1,0:T(8,128)(2,1)} %act.1, bf16[3,64,1024]{2,1,0:T(8,128)(2,1)} %w.1, f32[3,3,1024]{2,1,0:T(4,128)} %bitcast.1, f32[1024,256]{1,0:T(8,128)} %flt.1, bf16[1024,4096]{1,0:T(8,128)(2,1)} %w_out.1, bf16[128,128]{1,0:T(8,128)(2,1)} %constant.10.clone.ahead, ...), custom_call_target="tpu_custom_call" | custom-call | tf_op jit(solution)/shard_map/layer/pallas_call | solution.py:409
  133.3 1.9 %copy.12 = bf16[256,1024]{1,0:T(8,128)(2,1)} copy(bf16[256,1024]{1,0:T(8,128)(2,1)} %layer.1) | data formatting | bytes 1048576

commit v3 on v2

v3 whole, which is shorter than its diff:
```python
import math

import numpy as np
import ml_dtypes
import jax
import jax.numpy as jnp
from jax import lax
from jax.experimental import pallas as pl
from jax.experimental.pallas import tpu as pltpu
from jax.sharding import PartitionSpec as P

MESH = pl.DeviceIdType.MESH
BF = jnp.bfloat16
F32 = jnp.float32
TAPS = 3
NY, NX, NZ = 2, 4, 8
BLK = 256
HALO = 16
ROWS = BLK + HALO
D = 4096
CQ = 256
DB = 64


def place():
    ctx = lax.axis_index("ctx")
    hid = lax.axis_index("hid")
    yl = lax.div(ctx, 32)
    x = lax.rem(lax.div(ctx, 8), 4)
    z = lax.rem(ctx, 8)
    return ctx, hid, yl, x, z


def at_ctx(yl, x, z):
    return {"ctx": yl * 32 + x * 8 + z}


class Copies:
    def __init__(self, send, recv):
        self.send, self.recv, self.all = send, recv, []

    def start(self, src, dst, device):
        k = len(self.all)
        copy = pltpu.make_async_remote_copy(
            src_ref=src,
            dst_ref=dst,
            send_sem=self.send.at[k],
            recv_sem=self.recv.at[k],
            device_id=device,
            device_id_type=MESH,
        )
        copy.start()
        self.all.append(copy)
        return copy

    def wait_sends(self):
        for copy in self.all:
            copy.wait_send()


def halves(table):
    high = table.astype(ml_dtypes.bfloat16)
    low = (table - high.astype(np.float64)).astype(ml_dtypes.bfloat16)
    return high, low


def tables():
    order = np.array([yl * 32 + x * 8 + z for yl in range(NY) for z in range(NZ) for x in range(NX)])
    k1 = np.arange(64) + 0.5
    angle = 2 * np.pi * np.outer(k1, np.arange(64)) / 128
    ahead = np.concatenate([np.cos(angle), -np.sin(angle)], axis=0)
    back = np.concatenate([np.cos(angle.T), -np.sin(angle.T)], axis=1) * 2.0**-14
    turn = 2 * np.pi * np.outer(k1, np.arange(BLK)) / 32768
    inner = 2 * np.pi * (np.outer(np.arange(BLK), np.arange(BLK)) % BLK) / BLK
    c, s = np.cos(inner), np.sin(inner)
    wide = np.block([[c, -s], [s, c]])
    sides = np.array([part * BLK + side * 128 + i for side in range(2) for part in range(2) for i in range(128)])
    wide = wide[sides][:, sides]
    ahead_h, ahead_l = halves(ahead[:, order])
    back_h, back_l = halves(back[order])
    wide_h, wide_l = halves(wide)
    return (
        np.concatenate([ahead_h, ahead_l], axis=1),
        np.stack([np.cos(turn), -np.sin(turn)]).astype(np.float32),
        wide_h,
        wide_l,
        np.concatenate([back_h, back_h, back_l], axis=1),
    )


N_COPIES = 120
UNITS = {"b0": (0, 0, 3), "b1": (1, 0, 3), "b2": (3, 2, 1), "a0": (2, 0, 3), "a1": (3, 0, 2)}
GROUP = 4


def split(value):
    high = value.astype(BF)
    return high, (value - high.astype(F32)).astype(BF)


def layer_kernel(
    act, w, taps, flt, w_out, ahead, turn, wide_h, wide_l, back, out,
    abuf, wbuf, bs, f32buf, f16buf, fx, frecv, drv, drecv, qry, qrecv, wide, out32, spec, p_high, p_low, osend, crecv,
    obuf, psend, precv, ysend, yrecv, held, local_sem, own_sem, all_send, all_recv, send_sem, recv_sem,
):
    ctx, hid, yl, x, z = place()
    core = lax.rem(hid, 2)
    yh = lax.div(hid, 2)
    mate = {"hid": hid + 1 - 2 * core}
    across = {"hid": lax.rem(hid + 2, 4)}
    me = yl * NZ + z
    right, left = lax.rem(z + 1, NZ), lax.rem(z + NZ - 1, NZ)
    xr, xl, xo = lax.rem(x + 1, NX), lax.rem(x + 3, NX), lax.rem(x + 2, NX)
    after = lax.rem(ctx + 1, 64)
    to_r, to_l = at_ctx(yl, x, right), at_ctx(yl, x, left)
    to_y = at_ctx(1 - yl, x, z)
    to_xr, to_xl, to_xo = at_ctx(yl, xr, z), at_ctx(yl, xl, z), at_ctx(yl, xo, z)

    own_w = pltpu.make_async_copy(
        w.at[:, :, pl.ds(pl.multiple_of(x * CQ, CQ), CQ)], wbuf.at[:, yl, x, z], local_sem.at[0]
    )
    own_a = pltpu.make_async_copy(act, abuf.at[x, pl.ds(HALO, BLK)], local_sem.at[1])
    own_w.start()
    own_a.start()

    own_f = pltpu.make_async_copy(flt, f32buf, local_sem.at[2])
    own_f.start()
    own_o = [
        pltpu.make_async_copy(w_out.at[:, pl.ds(1024 * h, 1024)], obuf.at[h], local_sem.at[3 + h])
        for h in range(4)
    ]
    for copy in own_o:
        copy.start()

    own_f.wait()
    f16buf[...] = f32buf[...].astype(BF).reshape(NX, 16, 16, BLK)
    own_x = pltpu.make_async_copy(f16buf.at[x], fx.at[:, x], local_sem.at[2])
    own_x.start()
    barrier = pltpu.get_barrier_semaphore()

    def greet(t, carry):
        pl.semaphore_signal(barrier, inc=1, device_id={"ctx": lax.rem(ctx + t, 64)}, device_id_type=MESH)
        return carry

    lax.fori_loop(1, 64, greet, 0)
    for peer in (mate, across):
        pl.semaphore_signal(barrier, inc=1, device_id=peer, device_id_type=MESH)
    pl.semaphore_wait(barrier, 65)

    go = Copies(send_sem, recv_sem)

    def spread(src, dst, sem):
        def one(t, carry):
            p = lax.rem(me + t, 16)
            pltpu.make_async_remote_copy(
                src_ref=src(p),
                dst_ref=dst,
                send_sem=all_send.at[sem],
                recv_sem=all_recv.at[sem],
                device_id=at_ctx(lax.div(p, NZ), x, lax.rem(p, NZ)),
                device_id_type=MESH,
            ).start()
            return carry

        lax.fori_loop(1, 16, one, 0)

    def to_all(src, dst, sem):
        spread(lambda p: src.at[p], dst.at[me], sem)
        pltpu.make_async_copy(src.at[me], dst.at[me], own_sem.at[sem]).start()

    def await_all(src, dst, sem):
        pltpu.make_async_copy(src.at[me], dst.at[me], own_sem.at[sem]).wait()
        pltpu.make_async_copy(dst.at[pl.ds(0, 15)], dst.at[pl.ds(0, 15)], all_recv.at[sem]).wait()

    def sent_all(src, sem, count=15):
        pltpu.make_async_copy(src.at[pl.ds(0, count)], src.at[pl.ds(0, count)], all_send.at[sem]).wait()

    first = []
    for xp, to in ((xr, to_xr), (xl, to_xl), (xo, to_xo)):
        first.append(
            go.start(w.at[:, :, pl.ds(pl.multiple_of(xp * CQ, CQ), CQ)], wbuf.at[:, yl, x, z], to)
        )

    def unit(name, zs):
        ys = 1 - yl if name[0] == "p" else yl
        xs, j, count = UNITS[name.replace("p", "a")]
        return wbuf.at[pl.ds(j, count), ys, lax.rem(x + xs, NX), zs]

    def send(name, zs, to):
        part = unit(name, zs)
        return go.start(part, part, to)

    from_l, from_r, y_in = {}, {}, {}

    def send_own(name):
        from_l[name, 1] = send(name, z, to_r)
        from_r[name, 1] = send(name, z, to_l)

    own_w.wait()
    send_own("b0")
    y_in["b0"] = send("b0", z, to_y)
    x_next = lax.rem(lax.div(after, 8), 4)
    lanes = pl.ds(pl.multiple_of(core * (D // 2), D // 2), D // 2)
    halo_in = go.start(
        act.at[pl.ds(BLK - HALO, HALO), lanes], abuf.at[x_next, pl.ds(0, HALO), lanes], {"ctx": after}
    )
    first[1].wait_recv()
    send_own("b1")
    y_in["b1"] = send("b1", z, to_y)
    first[0].wait_recv()
    y_in["a1"] = send("a1", z, to_y)
    send_own("b2")
    y_in["b2"] = send("b2", z, to_y)
    first[2].wait_recv()
    y_in["a0"] = send("a0", z, to_y)
    send_own("a1")
    send_own("a0")

    def a_rows(part):
        return pl.multiple_of(core * 128 + part * 64, 64)

    def a_slot(block, part, count=64):
        return abuf.at[block, pl.ds(pl.multiple_of(HALO + core * 128 + part * 64, 16), count)]

    def a_send(part, to):
        return go.start(act.at[pl.ds(a_rows(part), 64)], a_slot(x, part), to)

    near = [a_send(0, to_xr), a_send(1, to_xl)]
    fx_in = [go.start(f16buf.at[xp], fx.at[:, x], to) for xp, to in ((xr, to_xr), (xl, to_xl), (xo, to_xo))]
    for name in ("a1", "a0"):
        y_in[name].wait_recv()
        send_own(name.replace("a", "p"))

    def relay(step):
        zl, zr = lax.rem(z + NZ - step, NZ), lax.rem(z + step, NZ)
        for name in ("b0", "b1", "b2", "a1", "a0", "p1", "p0"):
            for source, zs, to, last in ((from_l, zl, to_r, ("b0", "a1", "a0")), (from_r, zr, to_l, ("b1", "b2", "p1", "p0"))):
                source[name, step].wait_recv()
                if step < 3 or name in last:
                    source[name, step + 1] = send(name, zs, to)
                if name[0] == "b":
                    y_in[name, step, to is to_r] = send(name, zs, to_y)

    relay(1)
    near += [a_send(1, to_xr), a_send(0, to_xl)]
    near[0].wait_recv()
    far = [go.start(a_slot(xl, 0), a_slot(xl, 0), to_xr)]
    near[1].wait_recv()
    far.append(go.start(a_slot(xr, 1), a_slot(xr, 1), to_xl))
    halo_in.wait_recv()
    halo_own = abuf.at[x, pl.ds(0, HALO), lanes]
    halos = [go.start(halo_own, halo_own, to) for to in (to_xr, to_xl, to_xo)]
    mates = [go.start(a_slot(xl, 0), a_slot(xl, 0), mate), go.start(a_slot(xr, 1), a_slot(xr, 1), mate)]
    relay(2)
    for copy in halos:
        copy.wait_recv()
    halo_all = abuf.at[:, pl.ds(0, HALO), lanes]
    mates.append(go.start(halo_all, halo_all, mate))
    relay(3)
    for copy, block, part in ((near[2], xl, 1), (near[3], xr, 0), (far[0], xo, 0), (far[1], xo, 1)):
        copy.wait_recv()
        mates.append(go.start(a_slot(block, part), a_slot(block, part), mate))
    zo = lax.rem(z + 4, NZ)
    for name in ("b0", "b1", "b2", "a1", "p1", "a0", "p0"):
        (from_l if name in ("b0", "a1", "a0") else from_r)[name, 4].wait_recv()
        if name[0] == "b":
            y_in[name, 4] = send(name, zo, to_y)
    own_x.wait()
    for copy in fx_in:
        copy.wait_recv()
    to_all(fx, frecv, 1)
    for name, copy in y_in.items():
        if name not in ("a0", "a1"):
            copy.wait_recv()
    for copy in mates:
        copy.wait_recv()
    own_a.wait()

    def block(xb, carry):
        keep = jnp.where(yl * 32 + xb * 8 + z == 0, 0.0, 1.0).astype(F32)
        a = abuf[xb]
        filtered = []
        for j in range(3):
            wj = wbuf[j].reshape(D, CQ)
            bs[j] = jnp.dot(a, wj, preferred_element_type=F32).astype(BF).astype(F32)
            bs[j, pl.ds(0, HALO)] = bs[j, pl.ds(0, HALO)] * keep
            mine = pl.ds(pl.multiple_of(x * CQ, CQ), CQ)
            total = taps[j, pl.ds(0, 1), mine] * bs[j, pl.ds(HALO, BLK)]
            for k in range(1, TAPS):
                total = total + taps[j, pl.ds(k, 1), mine] * bs[j, pl.ds(HALO - k, BLK)]
            filtered.append(total)
        drv[:, xb] = (filtered[0] * filtered[2]).T.astype(BF).reshape(16, 16, BLK)
        spread(lambda p: drv.at[p, xb], drecv.at[me, xb], 0)
        qry[xb] = filtered[1].T.astype(BF)
        return carry

    lax.fori_loop(0, NX, block, 0)
    pltpu.make_async_copy(drv.at[me], drecv.at[me], own_sem.at[0]).start()
    own_q = pltpu.make_async_copy(qry.at[x], qrecv.at[x], local_sem.at[0])
    own_q.start()
    q_in = [go.start(qry.at[xp], qrecv.at[x], to) for xp, to in ((xr, to_xr), (xl, to_xl), (xo, to_xo))]

    def inner(high, low, columns):
        return (
            jnp.dot(high, wide_h[:, columns], preferred_element_type=F32)
            + jnp.dot(low, wide_h[:, columns], preferred_element_type=F32)
            + jnp.dot(high, wide_l[:, columns], preferred_element_type=F32)
        )

    def widen(source):
        for side in range(2):
            half = source[:, :, :, 128 * side : 128 * side + 128]
            wide[side] = half.astype(F32).reshape(1024, 128)

    def spectrum(first):
        parts = []
        for i in range(GROUP):
            rows = jnp.concatenate(
                [wide[side, pl.ds(first + i, 64, stride=16), :] for side in range(2)], axis=1
            ).astype(BF)
            both = jnp.dot(ahead[...], jnp.concatenate([rows, rows], axis=0), preferred_element_type=F32)
            pieces = []
            for side in range(2):
                at = slice(128 * side, 128 * side + 128)
                re, im, tr, ti = both[:64, at], both[64:, at], turn[0, :, at], turn[1, :, at]
                pieces += [re * tr - im * ti, re * ti + im * tr]
            parts.append(jnp.concatenate(pieces, axis=1))
        return inner(*split(jnp.concatenate(parts, axis=0)), slice(None))

    def filter_group(g, carry):
        spec[g] = spectrum(g * GROUP)
        return carry

    def signal_group(g, carry):
        s = spectrum(g * GROUP)
        for side in range(2):
            re, im = slice(256 * side, 256 * side + 128), slice(256 * side + 128, 256 * side + 256)
            sr, si, hr, hi = s[:, re], s[:, im], spec[g, :, re], spec[g, :, im]
            p_high[g, :, re], p_low[g, :, re] = split(sr * hr - si * hi)
            p_high[g, :, im], p_low[g, :, im] = split(-(sr * hi + si * hr))
        return carry

    def inverse_group(side):
        at = slice(128 * side, 128 * side + 128)

        def one(g, carry):
            v = inner(p_high[g], p_low[g], slice(256 * side, 256 * side + 256))
            for i in range(0, GROUP, 2):
                pair = []
                for c in (i, i + 1):
                    re, im = v[64 * c : 64 * c + 64, :128], -v[64 * c : 64 * c + 64, 128:]
                    tr, ti = turn[0, :, at], turn[1, :, at]
                    pair.append(jnp.concatenate([re * tr + im * ti, im * tr - re * ti], axis=0))
                high, low = split(jnp.concatenate(pair, axis=1))
                y = jnp.dot(back[...], jnp.concatenate([high, low, high], axis=0), preferred_element_type=F32)
                out32[side, pl.ds(g * GROUP + i, 64, stride=16), :] = y[:, :128]
                out32[side, pl.ds(g * GROUP + i + 1, 64, stride=16), :] = y[:, 128:]
            return carry

        return one

    await_all(fx, frecv, 1)
    widen(frecv)
    lax.fori_loop(0, 16 // GROUP, filter_group, 0)
    await_all(drv, drecv, 0)
    widen(drecv)
    lax.fori_loop(0, 16 // GROUP, signal_group, 0)

    slot = x * 16 + me
    own_c = []
    for side in range(2):
        lax.fori_loop(0, 16 // GROUP, inverse_group(side), 0)
        osend[side] = out32[side].reshape(64, 16, 128).astype(BF)

        def home(t, carry):
            c = lax.rem(ctx + t, 64)
            yt, xt, zt = lax.div(c, 32), lax.rem(lax.div(c, 8), 4), lax.rem(c, 8)
            pltpu.make_async_remote_copy(
                src_ref=osend.at[side, (yt * NZ + zt) * NX + xt],
                dst_ref=crecv.at[side, slot],
                send_sem=all_send.at[2 + side],
                recv_sem=all_recv.at[2 + side],
                device_id={"ctx": c},
                device_id_type=MESH,
            ).start()
            return carry

        lax.fori_loop(1, 64, home, 0)
        own_c.append(
            pltpu.make_async_copy(osend.at[side, me * NX + x], crecv.at[side, slot], own_sem.at[2 + side])
        )
        own_c[side].start()

    own_q.wait()
    for copy in q_in:
        copy.wait_recv()
    for copy in own_o:
        copy.wait()

    far_h, near_h = (1 - yh) * 2, yh * 2
    p_in, y_copy = {}, []
    for side in range(2):
        own_c[side].wait()
        arrived = crecv.at[side, pl.ds(0, 63)]
        pltpu.make_async_copy(arrived, arrived, all_recv.at[2 + side]).wait()
        query = qrecv[:, :, 128 * side : 128 * side + 128].reshape(1024, 128).astype(F32)
        gated = (query * crecv[side].reshape(1024, 128).astype(F32)).T.astype(BF)

        def partial(h):
            return jnp.dot(gated, obuf[h], preferred_element_type=F32)

        psend[side, 0] = partial(far_h + 1 - core).astype(BF)
        p_in[side, 0] = go.start(psend.at[side, 0], precv.at[side, 0], mate)
        total = partial(far_h + core)
        p_in[side, 0].wait_recv()
        ysend[side] = (total + precv[side, 0].astype(F32)).astype(BF)
        y_copy.append(go.start(ysend.at[side], yrecv.at[side], across))
        psend[side, 1] = partial(near_h + 1 - core).astype(BF)
        p_in[side, 1] = go.start(psend.at[side, 1], precv.at[side, 1], mate)
        held[side] = partial(near_h + core)
    for side in range(2):
        p_in[side, 1].wait_recv()
        y_copy[side].wait_recv()
        total = held[side] + precv[side, 1].astype(F32) + yrecv[side].astype(F32)
        out[pl.ds(128 * side, 128), :] = total.astype(BF)

    go.wait_sends()
    sent_all(drv, 0)
    sent_all(fx, 1)
    for side in range(2):
        sent_all(osend.at[side], 2 + side, 63)


def layer(act, w, taps, flt, w_out):
    any_space, vmem = pl.BlockSpec(memory_space=pl.ANY), pl.BlockSpec(memory_space=pltpu.VMEM)
    return pl.pallas_call(
        layer_kernel,
        out_shape=jax.ShapeDtypeStruct((BLK, 1024), BF),
        in_specs=[any_space, any_space, vmem, any_space, any_space] + [vmem] * 5,
        out_specs=vmem,
        scratch_shapes=[
            pltpu.VMEM((NX, ROWS, D), BF),
            pltpu.VMEM((3, NY, NX, NZ, DB, CQ), BF),
            pltpu.VMEM((3, ROWS, CQ), F32),
            pltpu.VMEM((1024, BLK), F32),
            pltpu.VMEM((NX, 16, 16, BLK), BF),
            pltpu.VMEM((16, NX, 16, BLK), BF),
            pltpu.VMEM((16, NX, 16, BLK), BF),
            pltpu.VMEM((16, NX, 16, BLK), BF),
            pltpu.VMEM((16, NX, 16, BLK), BF),
            pltpu.VMEM((NX, CQ, BLK), BF),
            pltpu.VMEM((NX, CQ, BLK), BF),
            pltpu.VMEM((2, 1024, 128), F32),
            pltpu.VMEM((2, 1024, 128), F32),
            pltpu.VMEM((16 // GROUP, 64 * GROUP, 2 * BLK), F32),
            pltpu.VMEM((16 // GROUP, 64 * GROUP, 2 * BLK), BF),
            pltpu.VMEM((16 // GROUP, 64 * GROUP, 2 * BLK), BF),
            pltpu.VMEM((2, 64, 16, 128), BF),
            pltpu.VMEM((2, 64, 16, 128), BF),
            pltpu.VMEM((4, 1024, 1024), BF),
            pltpu.VMEM((2, 2, 128, 1024), BF),
            pltpu.VMEM((2, 2, 128, 1024), BF),
            pltpu.VMEM((2, 128, 1024), BF),
            pltpu.VMEM((2, 128, 1024), BF),
            pltpu.VMEM((2, 128, 1024), F32),
            pltpu.SemaphoreType.DMA((8,)),
            pltpu.SemaphoreType.DMA((4,)),
            pltpu.SemaphoreType.DMA((4,)),
            pltpu.SemaphoreType.DMA((4,)),
            pltpu.SemaphoreType.DMA((N_COPIES,)),
            pltpu.SemaphoreType.DMA((N_COPIES,)),
        ],
        compiler_params=pltpu.CompilerParams(
            collective_id=0, has_side_effects=True, vmem_limit_bytes=58 * 1024 * 1024
        ),
        name="layer",
    )(act, w, taps, flt, w_out, *[jnp.asarray(table) for table in tables()])


def on_device(activations, w_in, short_taps, long_filter, w_out):
    return layer(activations, w_in, short_taps.transpose(0, 2, 1), long_filter, w_out)


def solution(mesh):
    return jax.shard_map(
        on_device,
        mesh=mesh,
        in_specs=(
            P("ctx", None),
            P(None, "ctx", "hid"),
            P(None, "hid", None),
            P("hid", "ctx"),
            P("hid", None),
        ),
        out_specs=P("ctx", "hid"),
        check_vma=False,
    )
```

time: 135 us -> 140 us (1.037)
  Pallas kernels: 133 us -> 138 us
    pallas_call x1, Pallas kernels: 133 us -> 138 us  [layer(): pl.pallas_call(layer_kernel, out_shape=jax.ShapeDtypeStruct((BLK, 1024),...]
where the time goes in v3:
time: 140 us
  Pallas kernels  138 us (99%)
  local copies, waits for them, and re-layouts  1.87 us (1%)
    pallas_call x1, Pallas kernels, layer(): pl.pallas_call(layer_kernel, out_shape=jax.ShapeDtypeStruct((BLK, 1024),...  138 us

profile of v3, /device:TPU:1, one launch (start us, length us, event | category | flops | bytes accessed | tf_op | source)
XLA Modules:
  0.0 139.8 jit_solution(16309146679993513550)
XLA Ops:
  0.0 138.0 %layer.1 = bf16[256,1024]{1,0:T(8,128)(2,1)} custom-call(bf16[256,4096]{1,0:T(8,128)(2,1)} %act.1, bf16[3,64,1024]{2,1,0:T(8,128)(2,1)} %w.1, f32[3,3,1024]{2,1,0:T(4,128)} %bitcast.1, f32[1024,256]{1,0:T(8,128)} %flt.1, bf16[1024,4096]{1,0:T(8,128)(2,1)} %w_out.1, bf16[128,128]{1,0:T(8,128)(2,1)} %constant.10.clone.ahead, ...), custom_call_target="tpu_custom_call" | custom-call | tf_op jit(solution)/shard_map/layer/pallas_call | solution.py:436
  138.0 1.9 %copy.12 = bf16[256,1024]{1,0:T(8,128)(2,1)} copy(bf16[256,1024]{1,0:T(8,128)(2,1)} %layer.1) | data formatting | bytes 1048576

commit v4 on v3

--- a/solution.py
+++ b/solution.py
@@ -99,10 +99,13 @@
 
 
 def layer_kernel(
-    act, w, taps, flt, w_out, ahead, turn, wide_h, wide_l, back, out,
-    abuf, wbuf, bs, f32buf, f16buf, fx, frecv, drv, drecv, qry, qrecv, wide, out32, spec, p_high, p_low, osend, crecv,
+    act, w, taps_in, flt, w_out, ahead_in, turn_in, wide_h_in, wide_l_in, back_in, out,
+    taps, ahead, turn, wide_h, wide_l, back, abuf, wbuf, bs, f32buf, f16buf, frecv, drv, drecv, qry, qrecv, wide, out32, spec, p_high, p_low, osend, crecv,
     obuf, psend, precv, ysend, yrecv, held, local_sem, own_sem, all_send, all_recv, send_sem, recv_sem,
 ):
+    tables_here = (
+        (taps_in, taps), (ahead_in, ahead), (turn_in, turn), (wide_h_in, wide_h), (wide_l_in, wide_l), (back_in, back)
+    )
     ctx, hid, yl, x, z = place()
     core = lax.rem(hid, 2)
     yh = lax.div(hid, 2)
@@ -111,7 +114,7 @@
     me = yl * NZ + z
     right, left = lax.rem(z + 1, NZ), lax.rem(z + NZ - 1, NZ)
     xr, xl, xo = lax.rem(x + 1, NX), lax.rem(x + 3, NX), lax.rem(x + 2, NX)
-    after = lax.rem(ctx + 1, 64)
+    after, before = lax.rem(ctx + 1, 64), lax.rem(ctx + 63, 64)
     to_r, to_l = at_ctx(yl, x, right), at_ctx(yl, x, left)
     to_y = at_ctx(1 - yl, x, z)
     to_xr, to_xl, to_xo = at_ctx(yl, xr, z), at_ctx(yl, xl, z), at_ctx(yl, xo, z)
@@ -123,29 +126,10 @@
     own_w.start()
     own_a.start()
 
-    own_f = pltpu.make_async_copy(flt, f32buf, local_sem.at[2])
-    own_f.start()
-    own_o = [
-        pltpu.make_async_copy(w_out.at[:, pl.ds(1024 * h, 1024)], obuf.at[h], local_sem.at[3 + h])
-        for h in range(4)
-    ]
-    for copy in own_o:
-        copy.start()
-
-    own_f.wait()
-    f16buf[...] = f32buf[...].astype(BF).reshape(NX, 16, 16, BLK)
-    own_x = pltpu.make_async_copy(f16buf.at[x], fx.at[:, x], local_sem.at[2])
-    own_x.start()
     barrier = pltpu.get_barrier_semaphore()
-
-    def greet(t, carry):
-        pl.semaphore_signal(barrier, inc=1, device_id={"ctx": lax.rem(ctx + t, 64)}, device_id_type=MESH)
-        return carry
-
-    lax.fori_loop(1, 64, greet, 0)
-    for peer in (mate, across):
+    for peer in (to_xr, to_xl, to_xo, to_r, to_l, to_y, mate, across, {"ctx": after}, {"ctx": before}):
         pl.semaphore_signal(barrier, inc=1, device_id=peer, device_id_type=MESH)
-    pl.semaphore_wait(barrier, 65)
+    pl.semaphore_wait(barrier, 10)
 
     go = Copies(send_sem, recv_sem)
 
@@ -163,17 +147,6 @@
             return carry
 
         lax.fori_loop(1, 16, one, 0)
-
-    def to_all(src, dst, sem):
-        spread(lambda p: src.at[p], dst.at[me], sem)
-        pltpu.make_async_copy(src.at[me], dst.at[me], own_sem.at[sem]).start()
-
-    def await_all(src, dst, sem):
-        pltpu.make_async_copy(src.at[me], dst.at[me], own_sem.at[sem]).wait()
-        pltpu.make_async_copy(dst.at[pl.ds(0, 15)], dst.at[pl.ds(0, 15)], all_recv.at[sem]).wait()
-
-    def sent_all(src, sem, count=15):
-        pltpu.make_async_copy(src.at[pl.ds(0, count)], src.at[pl.ds(0, count)], all_send.at[sem]).wait()
 
     first = []
     for xp, to in ((xr, to_xr), (xl, to_xl), (xo, to_xo)):
@@ -226,7 +199,15 @@
         return go.start(act.at[pl.ds(a_rows(part), 64)], a_slot(x, part), to)
 
     near = [a_send(0, to_xr), a_send(1, to_xl)]
-    fx_in = [go.start(f16buf.at[xp], fx.at[:, x], to) for xp, to in ((xr, to_xr), (xl, to_xl), (xo, to_xo))]
+    loads = [pltpu.make_async_copy(flt, f32buf, local_sem.at[2])]
+    for k, (table, kept) in enumerate(tables_here):
+        loads.append(pltpu.make_async_copy(table, kept, local_sem.at[7 + k]))
+    own_o = [
+        pltpu.make_async_copy(w_out.at[:, pl.ds(1024 * h, 1024)], obuf.at[h], local_sem.at[3 + h])
+        for h in range(4)
+    ]
+    for copy in loads + own_o:
+        copy.start()
     for name in ("a1", "a0"):
         y_in[name].wait_recv()
         send_own(name.replace("a", "p"))
@@ -240,9 +221,10 @@
                     source[name, step + 1] = send(name, zs, to)
                 if name[0] == "b":
                     y_in[name, step, to is to_r] = send(name, zs, to_y)
+            if step == 1 and name == "b0":
+                near.extend([a_send(1, to_xr), a_send(0, to_xl)])
 
     relay(1)
-    near += [a_send(1, to_xr), a_send(0, to_xl)]
     near[0].wait_recv()
     far = [go.start(a_slot(xl, 0), a_slot(xl, 0), to_xr)]
     near[1].wait_recv()
@@ -251,12 +233,40 @@
     halo_own = abuf.at[x, pl.ds(0, HALO), lanes]
     halos = [go.start(halo_own, halo_own, to) for to in (to_xr, to_xl, to_xo)]
     mates = [go.start(a_slot(xl, 0), a_slot(xl, 0), mate), go.start(a_slot(xr, 1), a_slot(xr, 1), mate)]
+    for copy in loads:
+        copy.wait()
+    f16buf[...] = f32buf[...].astype(BF).reshape(NX, 16, 16, BLK)
     relay(2)
     for copy in halos:
         copy.wait_recv()
     halo_all = abuf.at[:, pl.ds(0, HALO), lanes]
     mates.append(go.start(halo_all, halo_all, mate))
     relay(3)
+
+    def to_owners(src, dst, sem):
+        def one(t, carry):
+            c = lax.rem(ctx + t, 64)
+            yt, xt, zt = lax.div(c, 32), lax.rem(lax.div(c, 8), 4), lax.rem(c, 8)
+            pltpu.make_async_remote_copy(
+                src_ref=src(xt, yt * NZ + zt),
+                dst_ref=dst,
+                send_sem=all_send.at[sem],
+                recv_sem=all_recv.at[sem],
+                device_id={"ctx": c},
+                device_id_type=MESH,
+            ).start()
+            return carry
+
+        lax.fori_loop(1, 64, one, 0)
+        own = pltpu.make_async_copy(src(x, me), dst, own_sem.at[sem])
+        own.start()
+        return own
+
+    def from_owners(dst, sem):
+        arrived = dst.at[pl.ds(0, 63)]
+        pltpu.make_async_copy(arrived, arrived, all_recv.at[sem]).wait()
+
+    own_f = to_owners(lambda xt, at: f16buf.at[xt, at], frecv.at[me * NX + x], 1)
     for copy, block, part in ((near[2], xl, 1), (near[3], xr, 0), (far[0], xo, 0), (far[1], xo, 1)):
         copy.wait_recv()
         mates.append(go.start(a_slot(block, part), a_slot(block, part), mate))
@@ -265,10 +275,6 @@
         (from_l if name in ("b0", "a1", "a0") else from_r)[name, 4].wait_recv()
         if name[0] == "b":
             y_in[name, 4] = send(name, zo, to_y)
-    own_x.wait()
-    for copy in fx_in:
-        copy.wait_recv()
-    to_all(fx, frecv, 1)
     for name, copy in y_in.items():
         if name not in ("a0", "a1"):
             copy.wait_recv()
@@ -295,7 +301,8 @@
         return carry
 
     lax.fori_loop(0, NX, block, 0)
-    pltpu.make_async_copy(drv.at[me], drecv.at[me], own_sem.at[0]).start()
+    own_d = pltpu.make_async_copy(drv.at[me], drecv.at[me], own_sem.at[0])
+    own_d.start()
     own_q = pltpu.make_async_copy(qry.at[x], qrecv.at[x], local_sem.at[0])
     own_q.start()
     q_in = [go.start(qry.at[xp], qrecv.at[x], to) for xp, to in ((xr, to_xr), (xl, to_xl), (xo, to_xo))]
@@ -309,7 +316,7 @@
 
     def widen(source):
         for side in range(2):
-            half = source[:, :, :, 128 * side : 128 * side + 128]
+            half = source[:, :, 128 * side : 128 * side + 128]
             wide[side] = half.astype(F32).reshape(1024, 128)
 
     def spectrum(first):
@@ -359,11 +366,13 @@
 
         return one
 
-    await_all(fx, frecv, 1)
-    widen(frecv)
+    own_f.wait()
+    from_owners(frecv, 1)
+    widen(frecv[...])
     lax.fori_loop(0, 16 // GROUP, filter_group, 0)
-    await_all(drv, drecv, 0)
-    widen(drecv)
+    own_d.wait()
+    pltpu.make_async_copy(drecv.at[pl.ds(0, 15)], drecv.at[pl.ds(0, 15)], all_recv.at[0]).wait()
+    widen(drecv[...].reshape(64, 16, BLK))
     lax.fori_loop(0, 16 // GROUP, signal_group, 0)
 
     slot = x * 16 + me
@@ -372,24 +381,9 @@
         lax.fori_loop(0, 16 // GROUP, inverse_group(side), 0)
         osend[side] = out32[side].reshape(64, 16, 128).astype(BF)
 
-        def home(t, carry):
-            c = lax.rem(ctx + t, 64)
-            yt, xt, zt = lax.div(c, 32), lax.rem(lax.div(c, 8), 4), lax.rem(c, 8)
-            pltpu.make_async_remote_copy(
-                src_ref=osend.at[side, (yt * NZ + zt) * NX + xt],
-                dst_ref=crecv.at[side, slot],
-                send_sem=all_send.at[2 + side],
-                recv_sem=all_recv.at[2 + side],
-                device_id={"ctx": c},
-                device_id_type=MESH,
-            ).start()
-            return carry
-
-        lax.fori_loop(1, 64, home, 0)
         own_c.append(
-            pltpu.make_async_copy(osend.at[side, me * NX + x], crecv.at[side, slot], own_sem.at[2 + side])
+            to_owners(lambda xt, at, side=side: osend.at[side, at * NX + xt], crecv.at[side, slot], 2 + side)
         )
-        own_c[side].start()
 
     own_q.wait()
     for copy in q_in:
@@ -401,8 +395,7 @@
     p_in, y_copy = {}, []
     for side in range(2):
         own_c[side].wait()
-        arrived = crecv.at[side, pl.ds(0, 63)]
-        pltpu.make_async_copy(arrived, arrived, all_recv.at[2 + side]).wait()
+        from_owners(crecv.at[side], 2 + side)
         query = qrecv[:, :, 128 * side : 128 * side + 128].reshape(1024, 128).astype(F32)
         gated = (query * crecv[side].reshape(1024, 128).astype(F32)).T.astype(BF)
 
@@ -425,10 +418,11 @@
         out[pl.ds(128 * side, 128), :] = total.astype(BF)
 
     go.wait_sends()
-    sent_all(drv, 0)
-    sent_all(fx, 1)
+    pltpu.make_async_copy(drv.at[pl.ds(0, 15)], drv.at[pl.ds(0, 15)], all_send.at[0]).wait()
+    pltpu.make_async_copy(frecv.at[pl.ds(0, 63)], frecv.at[pl.ds(0, 63)], all_send.at[1]).wait()
     for side in range(2):
-        sent_all(osend.at[side], 2 + side, 63)
+        part = osend.at[side, pl.ds(0, 63)]
+        pltpu.make_async_copy(part, part, all_send.at[2 + side]).wait()
 
 
 def layer(act, w, taps, flt, w_out):
@@ -436,16 +430,21 @@
     return pl.pallas_call(
         layer_kernel,
         out_shape=jax.ShapeDtypeStruct((BLK, 1024), BF),
-        in_specs=[any_space, any_space, vmem, any_space, any_space] + [vmem] * 5,
+        in_specs=[any_space] * 10,
         out_specs=vmem,
         scratch_shapes=[
+            pltpu.VMEM((3, TAPS, 1024), F32),
+            pltpu.VMEM((128, 128), BF),
+            pltpu.VMEM((2, 64, BLK), F32),
+            pltpu.VMEM((2 * BLK, 2 * BLK), BF),
+            pltpu.VMEM((2 * BLK, 2 * BLK), BF),
+            pltpu.VMEM((64, 384), BF),
             pltpu.VMEM((NX, ROWS, D), BF),
             pltpu.VMEM((3, NY, NX, NZ, DB, CQ), BF),
             pltpu.VMEM((3, ROWS, CQ), F32),
             pltpu.VMEM((1024, BLK), F32),
             pltpu.VMEM((NX, 16, 16, BLK), BF),
-            pltpu.VMEM((16, NX, 16, BLK), BF),
-            pltpu.VMEM((16, NX, 16, BLK), BF),
+            pltpu.VMEM((64, 16, BLK), BF),
             pltpu.VMEM((16, NX, 16, BLK), BF),
             pltpu.VMEM((16, NX, 16, BLK), BF),
             pltpu.VMEM((NX, CQ, BLK), BF),
@@ -463,7 +462,7 @@
             pltpu.VMEM((2, 128, 1024), BF),
             pltpu.VMEM((2, 128, 1024), BF),
             pltpu.VMEM((2, 128, 1024), F32),
-            pltpu.SemaphoreType.DMA((8,)),
+            pltpu.SemaphoreType.DMA((16,)),
             pltpu.SemaphoreType.DMA((4,)),
             pltpu.SemaphoreType.DMA((4,)),
             pltpu.SemaphoreType.DMA((4,)),

time: 140 us -> 131 us (0.936)
  Pallas kernels: 138 us -> 129 us
    pallas_call x1, Pallas kernels: 138 us -> 129 us  [layer(): pl.pallas_call(layer_kernel, out_shape=jax.ShapeDtypeStruct((BLK, 1024),...]
where the time goes in v4:
time: 131 us; the launch traced here: 130 us
  Pallas kernels  129 us (98%)
  local copies, waits for them, and re-layouts  1.87 us (1%)
    pallas_call x1, Pallas kernels, layer(): pl.pallas_call(layer_kernel, out_shape=jax.ShapeDtypeStruct((BLK, 1024),...  129 us

profile of v4, /device:TPU:1, one launch (start us, length us, event | category | flops | bytes accessed | tf_op | source)
XLA Modules:
  0.0 130.5 jit_solution(5156734974771778222)
XLA Ops:
  0.0 128.6 %layer.1 = bf16[256,1024]{1,0:T(8,128)(2,1)} custom-call(bf16[256,4096]{1,0:T(8,128)(2,1)} %act.1, bf16[3,64,1024]{2,1,0:T(8,128)(2,1)} %w.1, f32[3,3,1024]{2,1,0:T(4,128)} %bitcast.1, f32[1024,256]{1,0:T(8,128)} %flt.1, bf16[1024,4096]{1,0:T(8,128)(2,1)} %w_out.1, bf16[128,128]{1,0:T(8,128)(2,1)} %constant.10.clone.ahead_in, ...), custom_call_target="tpu_custom_call" | custom-call | tf_op jit(solution)/shard_map/layer/pallas_call | solution.py:430
  128.6 1.9 %copy.12 = bf16[256,1024]{1,0:T(8,128)(2,1)} copy(bf16[256,1024]{1,0:T(8,128)(2,1)} %layer.1) | data formatting | bytes 1048576

commit v5 on v4

--- a/solution.py
+++ b/solution.py
@@ -169,6 +169,15 @@
         from_l[name, 1] = send(name, z, to_r)
         from_r[name, 1] = send(name, z, to_l)
 
+    loads = [pltpu.make_async_copy(flt, f32buf, local_sem.at[2])]
+    for k, (table, kept) in enumerate(tables_here):
+        loads.append(pltpu.make_async_copy(table, kept, local_sem.at[7 + k]))
+    own_o = [
+        pltpu.make_async_copy(w_out.at[:, pl.ds(1024 * h, 1024)], obuf.at[h], local_sem.at[3 + h])
+        for h in range(4)
+    ]
+    for copy in loads:
+        copy.start()
     own_w.wait()
     send_own("b0")
     y_in["b0"] = send("b0", z, to_y)
@@ -199,18 +208,24 @@
         return go.start(act.at[pl.ds(a_rows(part), 64)], a_slot(x, part), to)
 
     near = [a_send(0, to_xr), a_send(1, to_xl)]
-    loads = [pltpu.make_async_copy(flt, f32buf, local_sem.at[2])]
-    for k, (table, kept) in enumerate(tables_here):
-        loads.append(pltpu.make_async_copy(table, kept, local_sem.at[7 + k]))
-    own_o = [
-        pltpu.make_async_copy(w_out.at[:, pl.ds(1024 * h, 1024)], obuf.at[h], local_sem.at[3 + h])
-        for h in range(4)
-    ]
-    for copy in loads + own_o:
-        copy.start()
+    for copy in loads:
+        copy.wait()
+    f16buf[...] = f32buf[...].astype(BF).reshape(NX, 16, 16, BLK)
     for name in ("a1", "a0"):
         y_in[name].wait_recv()
         send_own(name.replace("a", "p"))
+    far, halos, mates = [], [], []
+
+    def far_half():
+        near[0].wait_recv()
+        far.append(go.start(a_slot(xl, 0), a_slot(xl, 0), to_xr))
+        near[1].wait_recv()
+        far.append(go.start(a_slot(xr, 1), a_slot(xr, 1), to_xl))
+        halo_in.wait_recv()
+        halo_own = abuf.at[x, pl.ds(0, HALO), lanes]
+        halos.extend([go.start(halo_own, halo_own, to) for to in (to_xr, to_xl, to_xo)])
+        for block, part in ((xl, 0), (xr, 1)):
+            mates.append(go.start(a_slot(block, part), a_slot(block, part), mate))
 
     def relay(step):
         zl, zr = lax.rem(z + NZ - step, NZ), lax.rem(z + step, NZ)
@@ -223,25 +238,18 @@
                     y_in[name, step, to is to_r] = send(name, zs, to_y)
             if step == 1 and name == "b0":
                 near.extend([a_send(1, to_xr), a_send(0, to_xl)])
+            if step == 2 and name == "a0":
+                far_half()
 
     relay(1)
-    near[0].wait_recv()
-    far = [go.start(a_slot(xl, 0), a_slot(xl, 0), to_xr)]
-    near[1].wait_recv()
-    far.append(go.start(a_slot(xr, 1), a_slot(xr, 1), to_xl))
-    halo_in.wait_recv()
-    halo_own = abuf.at[x, pl.ds(0, HALO), lanes]
-    halos = [go.start(halo_own, halo_own, to) for to in (to_xr, to_xl, to_xo)]
-    mates = [go.start(a_slot(xl, 0), a_slot(xl, 0), mate), go.start(a_slot(xr, 1), a_slot(xr, 1), mate)]
-    for copy in loads:
-        copy.wait()
-    f16buf[...] = f32buf[...].astype(BF).reshape(NX, 16, 16, BLK)
+    for copy in own_o:
+        copy.start()
     relay(2)
+    relay(3)
     for copy in halos:
         copy.wait_recv()
     halo_all = abuf.at[:, pl.ds(0, HALO), lanes]
-    mates.append(go.start(halo_all, halo_all, mate))
-    relay(3)
+    halo_mate = go.start(halo_all, halo_all, mate)
 
     def to_owners(src, dst, sem):
         def one(t, carry):
@@ -266,20 +274,21 @@
         arrived = dst.at[pl.ds(0, 63)]
         pltpu.make_async_copy(arrived, arrived, all_recv.at[sem]).wait()
 
+    zo = lax.rem(z + 4, NZ)
+    last = {"b0": from_l, "b1": from_r, "b2": from_r, "a1": from_l, "a0": from_l, "p1": from_r, "p0": from_r}
+    for name in ("b0", "b1", "b2"):
+        last[name][name, 4].wait_recv()
+        y_in[name, 4] = send(name, zo, to_y)
     own_f = to_owners(lambda xt, at: f16buf.at[xt, at], frecv.at[me * NX + x], 1)
     for copy, block, part in ((near[2], xl, 1), (near[3], xr, 0), (far[0], xo, 0), (far[1], xo, 1)):
         copy.wait_recv()
         mates.append(go.start(a_slot(block, part), a_slot(block, part), mate))
-    zo = lax.rem(z + 4, NZ)
-    for name in ("b0", "b1", "b2", "a1", "p1", "a0", "p0"):
-        (from_l if name in ("b0", "a1", "a0") else from_r)[name, 4].wait_recv()
-        if name[0] == "b":
-            y_in[name, 4] = send(name, zo, to_y)
+    for name in ("a1", "a0", "p1", "p0"):
+        last[name][name, 4].wait_recv()
     for name, copy in y_in.items():
         if name not in ("a0", "a1"):
             copy.wait_recv()
-    for copy in mates:
-        copy.wait_recv()
+    halo_mate.wait_recv()
     own_a.wait()
 
     def block(xb, carry):
@@ -300,7 +309,10 @@
         qry[xb] = filtered[1].T.astype(BF)
         return carry
 
-    lax.fori_loop(0, NX, block, 0)
+    block(x, 0)
+    for copy in mates:
+        copy.wait_recv()
+    lax.fori_loop(1, NX, lambda t, carry: block(lax.rem(x + t, NX), carry), 0)
     own_d = pltpu.make_async_copy(drv.at[me], drecv.at[me], own_sem.at[0])
     own_d.start()
     own_q = pltpu.make_async_copy(qry.at[x], qrecv.at[x], local_sem.at[0])

time: 131 us -> 120 us (0.916)
  Pallas kernels: 129 us -> 118 us
    pallas_call x1, Pallas kernels: 129 us -> 118 us  [layer(): pl.pallas_call(layer_kernel, out_shape=jax.ShapeDtypeStruct((BLK, 1024),...]
where the time goes in v5:
time: 120 us
  Pallas kernels  118 us (98%)
  local copies, waits for them, and re-layouts  1.87 us (2%)
    pallas_call x1, Pallas kernels, layer(): pl.pallas_call(layer_kernel, out_shape=jax.ShapeDtypeStruct((BLK, 1024),...  118 us

profile of v5, /device:TPU:1, one launch (start us, length us, event | category | flops | bytes accessed | tf_op | source)
XLA Modules:
  0.0 119.5 jit_solution(1834575465677914680)
XLA Ops:
  0.0 117.7 %layer.1 = bf16[256,1024]{1,0:T(8,128)(2,1)} custom-call(bf16[256,4096]{1,0:T(8,128)(2,1)} %act.1, bf16[3,64,1024]{2,1,0:T(8,128)(2,1)} %w.1, f32[3,3,1024]{2,1,0:T(4,128)} %bitcast.1, f32[1024,256]{1,0:T(8,128)} %flt.1, bf16[1024,4096]{1,0:T(8,128)(2,1)} %w_out.1, bf16[128,128]{1,0:T(8,128)(2,1)} %constant.10.clone.ahead_in, ...), custom_call_target="tpu_custom_call" | custom-call | tf_op jit(solution)/shard_map/layer/pallas_call | solution.py:442
  117.7 1.9 %copy.12 = bf16[256,1024]{1,0:T(8,128)(2,1)} copy(bf16[256,1024]{1,0:T(8,128)(2,1)} %layer.1) | data formatting | bytes 1048576

commit v6 on v5

v6 whole, which is shorter than its diff:
```python
import math

import numpy as np
import ml_dtypes
import jax
import jax.numpy as jnp
from jax import lax
from jax.experimental import pallas as pl
from jax.experimental.pallas import tpu as pltpu
from jax.sharding import PartitionSpec as P

MESH = pl.DeviceIdType.MESH
BF = jnp.bfloat16
F32 = jnp.float32
TAPS = 3
NY, NX, NZ = 2, 4, 8
BLK = 256
D = 4096
CG = 128
DB = 64


HOOK = 3


def place():
    ctx = lax.axis_index("ctx")
    hid = lax.axis_index("hid")
    yl = lax.div(ctx, 32)
    x = lax.rem(lax.div(ctx, 8), 4)
    z = lax.rem(ctx, 8)
    return ctx, hid, yl, x, z


def at_ctx(yl, x, z):
    return {"ctx": yl * 32 + x * 8 + z}


class Copies:
    def __init__(self, send, recv):
        self.send, self.recv, self.all = send, recv, []

    def start(self, src, dst, device):
        k = len(self.all)
        copy = pltpu.make_async_remote_copy(
            src_ref=src,
            dst_ref=dst,
            send_sem=self.send.at[k],
            recv_sem=self.recv.at[k],
            device_id=device,
            device_id_type=MESH,
        )
        copy.start()
        self.all.append(copy)
        return copy

    def wait_sends(self):
        for copy in self.all:
            copy.wait_send()


def halves(table):
    high = table.astype(ml_dtypes.bfloat16)
    low = (table - high.astype(np.float64)).astype(ml_dtypes.bfloat16)
    return high, low


def tables():
    order = np.array([yl * 32 + x * 8 + z for z in range(NZ) for yl in range(NY) for x in range(NX)])
    k1 = np.arange(64) + 0.5
    angle = 2 * np.pi * np.outer(k1, np.arange(64)) / 128
    ahead = np.concatenate([np.cos(angle), -np.sin(angle)], axis=0)
    back = np.concatenate([np.cos(angle.T), -np.sin(angle.T)], axis=1) * 2.0**-14
    turn = 2 * np.pi * np.outer(k1, np.arange(BLK)) / 32768
    inner = 2 * np.pi * (np.outer(np.arange(BLK), np.arange(BLK)) % BLK) / BLK
    c, s = np.cos(inner), np.sin(inner)
    wide = np.block([[c, -s], [s, c]])
    sides = np.array([part * BLK + side * 128 + i for side in range(2) for part in range(2) for i in range(128)])
    wide = wide[sides][:, sides]
    ahead_h, ahead_l = halves(ahead[:, order])
    back_h, back_l = halves(back[order])
    wide_h, wide_l = halves(wide)
    return (
        np.concatenate([ahead_h, ahead_l], axis=1),
        np.stack([np.cos(turn), -np.sin(turn)]).astype(np.float32),
        wide_h,
        wide_l,
        np.concatenate([back_h, back_l], axis=1),
    )


N_COPIES = 160
PLANE = [(0, 0), (1, 0), (0, 1), (0, 3), (0, 2), (1, 1), (1, 3), (1, 2)]
GROUP = 4


def split(value):
    high = value.astype(BF)
    return high, (value - high.astype(F32)).astype(BF)


def layer_kernel(
    act, w, taps_in, flt, w_out, ahead_in, turn_in, wide_h_in, wide_l_in, back_in, out,
    taps, ahead, turn, wide_h, wide_l, back, abuf, wbuf, last16, packed, halo_out, halo_in, halo_act, halo_br, bs, f32buf, f16buf, frecv, drv, drecv, qry, qrecv, wide, out32, spec, prod, osend, crecv,
    obuf, psend, precv, ysend, yrecv, held, local_sem, own_sem, all_send, all_recv, send_sem, recv_sem,
):
    tables_here = (
        (taps_in, taps), (ahead_in, ahead), (turn_in, turn), (wide_h_in, wide_h), (wide_l_in, wide_l), (back_in, back)
    )
    ctx, hid, yl, x, z = place()
    core = lax.rem(hid, 2)
    yh = lax.div(hid, 2)
    mate = {"hid": hid + 1 - 2 * core}
    across = {"hid": lax.rem(hid + 2, 4)}
    xr, xl, xo = lax.rem(x + 1, NX), lax.rem(x + 3, NX), lax.rem(x + 2, NX)
    after, before = lax.rem(z + 1, NZ), lax.rem(z + NZ - 1, NZ)
    to_r, to_l = at_ctx(yl, x, after), at_ctx(yl, x, before)
    to_xr, to_xl = at_ctx(yl, xr, z), at_ctx(yl, xl, z)
    to_s = at_ctx(1 - yl, x, z)
    to_o = {"ctx": (1 - yl) * 32 + x * 8 + z, "hid": lax.rem(hid + 2, 4)}
    mine = x * NY + yl

    def rel(dy, dx):
        return lax.rem(yl + dy, NY), lax.rem(x + dx, NX)

    def columns(y, xs):
        return pl.ds(pl.multiple_of((xs * NY + y) * CG, CG), CG)

    own_w = [
        pltpu.make_async_copy(
            w.at[j, :, columns(yl, x)], wbuf.at[yl, x, z, :, pl.ds(j * CG, CG)], local_sem.at[13 + j]
        )
        for j in range(3)
    ]
    own_a = pltpu.make_async_copy(act, abuf.at[yl, x], local_sem.at[1])
    tail = pltpu.make_async_copy(act.at[pl.ds(BLK - 16, 16)], last16, local_sem.at[0])
    for copy in own_w + [tail, own_a]:
        copy.start()

    barrier = pltpu.get_barrier_semaphore()
    peers = [mate, across, to_o] + [at_ctx(*rel(dy, dx), z) for dy, dx in PLANE[1:]]
    for dy, dx in PLANE:
        peers += [at_ctx(*rel(dy, dx), after), at_ctx(*rel(dy, dx), before)]
    for peer in peers:
        pl.semaphore_signal(barrier, inc=1, device_id=peer, device_id_type=MESH)
    pl.semaphore_wait(barrier, len(peers))

    go = Copies(send_sem, recv_sem)
    first = {}
    for dy, dx in PLANE[1:]:
        yt, xt = rel(dy, dx)
        first[dy, (NX - dx) % NX] = [
            go.start(
                w.at[j, :, columns(yt, xt)], wbuf.at[yl, x, z, :, pl.ds(j * CG, CG)], at_ctx(yt, xt, z)
            )
            for j in range(3)
        ]

    def send(unit, zs, to):
        yu, xu = rel(*unit)
        part = wbuf.at[yu, xu, zs]
        return go.start(part, part, to)

    from_l, from_r = {}, {}

    def send_own(unit):
        from_l[unit, 1] = send(unit, z, to_r)
        from_r[unit, 1] = send(unit, z, to_l)

    loads = [pltpu.make_async_copy(flt, f32buf, local_sem.at[2])]
    for k, (table, kept) in enumerate(tables_here):
        loads.append(pltpu.make_async_copy(table, kept, local_sem.at[7 + k]))
    own_o = [
        pltpu.make_async_copy(w_out.at[:, pl.ds(1024 * h, 1024)], obuf.at[h], local_sem.at[3 + h])
        for h in range(4)
    ]
    for copy in loads:
        copy.start()
    for copy in own_w:
        copy.wait()
    send_own((0, 0))

    tail.wait()
    rows = last16[...].astype(F32)
    for k in range(8):
        packed[pl.ds(2 * k, 2), :] = rows[14:16, 512 * k : 512 * k + 512]
    halo_out[...] = packed[...].astype(BF)
    halos = []
    x_next = lax.rem(x + lax.div(z + 1, NZ), NX)
    y_next = lax.rem(yl + lax.div(x * NZ + z + 1, NX * NZ), NY)
    for dy, dx in PLANE:
        halos.append(go.start(halo_out, halo_in.at[y_next, x_next], at_ctx(*rel(dy, dx), after)))

    for unit in PLANE[1:]:
        for copy in first[unit]:
            copy.wait_recv()
        send_own(unit)

    def a_slot(y, block, part, first_row=0, count=64):
        return abuf.at[y, block, pl.ds(pl.multiple_of(core * 128 + part * 64 + first_row, 16), count)]

    def a_send(part, to):
        return go.start(
            act.at[pl.ds(pl.multiple_of(core * 128 + part * 64, 64), 64)], a_slot(yl, x, part), to
        )

    y_in, mates = {}, {}

    def y_send(block, dx, part, count=32):
        for half, to in ((0, to_s), (1, to_o)):
            piece = a_slot(yl, block, part, half * count, count)
            y_in[dx, part, half] = go.start(piece, piece, to)

    def mate_own(block, dx, part):
        mates[0, dx, part] = go.start(a_slot(yl, block, part), a_slot(yl, block, part), mate)

    def mate_other(block, dx, part):
        y_in[dx, part, 0].wait_recv()
        y_in[dx, part, 1].wait_recv()
        if dx == 2:
            far_other[part].wait_recv()
        mates[1, dx, part] = go.start(a_slot(1 - yl, block, part), a_slot(1 - yl, block, part), mate)

    near = [a_send(0, to_xr), a_send(1, to_xl)]
    own_a.wait()
    y_send(x, 0, 0)
    y_send(x, 0, 1)
    for copy in loads:
        copy.wait()
    f16buf[...] = f32buf[...].astype(BF).reshape(8, NZ, 16, BLK)

    def relay(step):
        zl, zr = lax.rem(z + NZ - step, NZ), lax.rem(z + step, NZ)
        for k, unit in enumerate(PLANE):
            from_l[unit, step].wait_recv()
            if step < 3 or k % 2 == 0:
                from_l[unit, step + 1] = send(unit, zl, to_r)
            from_r[unit, step].wait_recv()
            if step < 3 or k % 2 == 1:
                from_r[unit, step + 1] = send(unit, zr, to_l)
            if k == HOOK and step in hooks:
                hooks[step]()

    def first_halves():
        near[0].wait_recv()
        y_send(xl, 3, 0)
        mate_own(xl, 3, 0)
        near[1].wait_recv()
        y_send(xr, 1, 1)
        mate_own(xr, 1, 1)
        far.append(go.start(a_slot(yl, xl, 0), a_slot(yl, xl, 0), to_xr))
        far.append(go.start(a_slot(yl, xr, 1), a_slot(yl, xr, 1), to_xl))

    def second_halves():
        near[2].wait_recv()
        y_send(xl, 3, 1)
        mate_own(xl, 3, 1)
        near[3].wait_recv()
        y_send(xr, 1, 0)
        mate_own(xr, 1, 0)

    far, far_other, hooks = [], [], {2: first_halves, 3: second_halves}
    relay(1)
    near += [a_send(1, to_xr), a_send(0, to_xl)]
    for copy in own_o:
        copy.start()
    relay(2)
    mate_other(x, 0, 0)
    mate_other(x, 0, 1)
    for copy in halos:
        copy.wait_recv()
    for y in range(NY):
        for xs in range(NX):
            got = halo_in[y, xs].astype(F32)
            for k in range(8):
                halo_act[pl.ds(2 * (y * NX + xs), 2), pl.ds(512 * k, 512)] = got[2 * k : 2 * k + 2]
    relay(3)
    mate_other(xl, 3, 0)
    mate_other(xr, 1, 1)
    for block, part, to in ((xl, 0, to_xr), (xr, 1, to_xl)):
        piece = a_slot(1 - yl, block, part, 32, 32)
        far_other.append(go.start(piece, piece, to))

    def to_owners(src, dst, sem):
        def one(t, carry):
            c = lax.rem(ctx + t, 64)
            yt, xt, zt = lax.div(c, 32), lax.rem(lax.div(c, 8), 4), lax.rem(c, 8)
            pltpu.make_async_remote_copy(
                src_ref=src(yt, xt, zt),
                dst_ref=dst,
                send_sem=all_send.at[sem],
                recv_sem=all_recv.at[sem],
                device_id={"ctx": c},
                device_id_type=MESH,
            ).start()
            return carry

        lax.fori_loop(1, 64, one, 0)
        own = pltpu.make_async_copy(src(yl, x, z), dst, own_sem.at[sem])
        own.start()
        return own

    def from_owners(dst, sem):
        arrived = dst.at[pl.ds(0, 63)]
        pltpu.make_async_copy(arrived, arrived, all_recv.at[sem]).wait()

    here = z * 8 + yl * NX + x
    own_f = to_owners(lambda yt, xt, zt: f16buf.at[xt * NY + yt, zt], frecv.at[here], 1)
    for k, unit in enumerate(PLANE):
        (from_l if k % 2 == 0 else from_r)[unit, 4].wait_recv()
    def await_mates(keys):
        for key in keys:
            for part in range(2):
                mates[(*key, part)].wait_recv()

    rims = jnp.dot(
        halo_act[...].astype(BF), wbuf[...].reshape(D, 3 * CG), preferred_element_type=F32
    ).astype(BF).astype(F32)
    halo_br[...] = jnp.zeros_like(halo_br)
    for b in range(8):
        halo_br[b, pl.ds(6, 2)] = rims[2 * b : 2 * b + 2]

    def block(yb, xb):
        at = yb * NX + xb
        keep = jnp.where(yb * 32 + xb * 8 + z == 0, 0.0, 1.0).astype(F32)
        bs[pl.ds(8, BLK)] = (
            jnp.dot(abuf[yb, xb], wbuf[...].reshape(D, 3 * CG), preferred_element_type=F32).astype(BF).astype(F32)
        )
        bs[pl.ds(0, 8)] = halo_br[at] * keep
        filtered = []
        for j in range(3):
            lanes = slice(j * CG, j * CG + CG)
            total = taps[j, pl.ds(0, 1), columns(yl, x)] * bs[pl.ds(8, BLK), lanes]
            for k in range(1, TAPS):
                total = total + taps[j, pl.ds(k, 1), columns(yl, x)] * bs[pl.ds(8 - k, BLK), lanes]
            filtered.append(total)
        drv[:, at] = (filtered[0] * filtered[2]).T.astype(BF).reshape(NZ, 16, BLK)

        def one(t, carry):
            zt = lax.rem(z + t, NZ)
            pltpu.make_async_remote_copy(
                src_ref=drv.at[zt, at],
                dst_ref=drecv.at[z, at],
                send_sem=all_send.at[0],
                recv_sem=all_recv.at[0],
                device_id=at_ctx(yl, x, zt),
                device_id_type=MESH,
            ).start()
            return carry

        lax.fori_loop(1, NZ, one, 0)
        qry[at] = filtered[1].T.astype(BF)

    def early(t, carry):
        block(lax.rem(yl + lax.div(t, 3), NY), lax.rem(x + t + lax.div(t, 2), NX))
        return carry

    def middle(t, carry):
        block(1 - yl, lax.rem(x + 1 + 2 * t, NX))
        return carry

    await_mates([(0, 1), (0, 3), (1, 0)])
    lax.fori_loop(0, 2, early, 0)
    for part in range(2):
        far[part].wait_recv()
        y_send(xo, 2, part, 16)
        mate_own(xo, 2, part)
    lax.fori_loop(2, 4, early, 0)


    mate_other(xl, 3, 1)
    mate_other(xr, 1, 0)
    await_mates([(1, 1), (1, 3), (0, 2)])
    lax.fori_loop(0, 2, middle, 0)
    block(yl, xo)
    mate_other(xo, 2, 0)
    mate_other(xo, 2, 1)
    await_mates([(1, 2)])
    block(1 - yl, xo)

    own_d = pltpu.make_async_copy(drv.at[z], drecv.at[z], own_sem.at[0])
    own_d.start()
    own_q = pltpu.make_async_copy(qry.at[yl * NX + x], qrecv.at[mine], local_sem.at[0])
    own_q.start()
    q_in = []
    for dy, dx in PLANE[1:]:
        yt, xt = rel(dy, dx)
        q_in.append(go.start(qry.at[yt * NX + xt], qrecv.at[mine], at_ctx(yt, xt, z)))

    def inner(high, columns):
        return jnp.dot(high, wide_h[:, columns], preferred_element_type=F32)

    def widen(source):
        for side in range(2):
            half = source[:, :, 128 * side : 128 * side + 128]
            wide[side] = half.astype(F32).reshape(1024, 128)

    def turned(first):
        parts = []
        for i in range(GROUP):
            rows = jnp.concatenate(
                [wide[side, pl.ds(first + i, 64, stride=16), :] for side in range(2)], axis=1
            ).astype(BF)
            both = jnp.dot(ahead[...], jnp.concatenate([rows, rows], axis=0), preferred_element_type=F32)
            pieces = []
            for side in range(2):
                at = slice(128 * side, 128 * side + 128)
                re, im, tr, ti = both[:64, at], both[64:, at], turn[0, :, at], turn[1, :, at]
                pieces += [re * tr - im * ti, re * ti + im * tr]
            parts.append(jnp.concatenate(pieces, axis=1))
        return jnp.concatenate(parts, axis=0)

    def filter_group(g, carry):
        high, low = split(turned(g * GROUP))
        spec[g] = (
            inner(high, slice(None))
            + inner(low, slice(None))
            + jnp.dot(high, wide_l[...], preferred_element_type=F32)
        )
        return carry

    def signal_group(g, carry):
        s = inner(turned(g * GROUP).astype(BF), slice(None))
        for side in range(2):
            re, im = slice(256 * side, 256 * side + 128), slice(256 * side + 128, 256 * side + 256)
            sr, si, hr, hi = s[:, re], s[:, im], spec[g, :, re], spec[g, :, im]
            prod[g, :, re] = (sr * hr - si * hi).astype(BF)
            prod[g, :, im] = -(sr * hi + si * hr).astype(BF)
        return carry

    def inverse_group(side):
        at = slice(128 * side, 128 * side + 128)

        def one(g, carry):
            v = inner(prod[g], slice(256 * side, 256 * side + 256))
            for i in range(0, GROUP, 2):
                pair = []
                for c in (i, i + 1):
                    re, im = v[64 * c : 64 * c + 64, :128], -v[64 * c : 64 * c + 64, 128:]
                    tr, ti = turn[0, :, at], turn[1, :, at]
                    pair.append(jnp.concatenate([re * tr + im * ti, im * tr - re * ti], axis=0))
                high = jnp.concatenate(pair, axis=1).astype(BF)
                y = jnp.dot(back[...], jnp.concatenate([high, high], axis=0), preferred_element_type=F32)
                out32[side, pl.ds(g * GROUP + i, 64, stride=16), :] = y[:, :128]
                out32[side, pl.ds(g * GROUP + i + 1, 64, stride=16), :] = y[:, 128:]
            return carry

        return one

    own_f.wait()
    from_owners(frecv, 1)
    widen(frecv[...])
    lax.fori_loop(0, 16 // GROUP, filter_group, 0)
    own_d.wait()
    pltpu.make_async_copy(drecv.at[pl.ds(0, 7)], drecv.at[pl.ds(0, 7)], all_recv.at[0]).wait()
    widen(drecv[...].reshape(64, 16, BLK))
    lax.fori_loop(0, 16 // GROUP, signal_group, 0)

    slot = mine * NZ + z
    own_c = []
    for side in range(2):
        lax.fori_loop(0, 16 // GROUP, inverse_group(side), 0)
        osend[side] = out32[side].reshape(64, 16, 128).astype(BF)

        own_c.append(
            to_owners(
                lambda yt, xt, zt, side=side: osend.at[side, zt * 8 + yt * NX + xt],
                crecv.at[side, slot],
                2 + side,
            )
        )

    own_q.wait()
    for copy in q_in:
        copy.wait_recv()
    for copy in own_o:
        copy.wait()

    far_h, near_h = (1 - yh) * 2, yh * 2
    p_in, y_copy = {}, {}
    for side in range(2):
        own_c[side].wait()
        from_owners(crecv.at[side], 2 + side)
        query = qrecv[:, :, 128 * side : 128 * side + 128].reshape(1024, 128).astype(F32)
        gated = (query * crecv[side].reshape(1024, 128).astype(F32)).T.astype(BF)

        def partial(h, half):
            return jnp.dot(gated, obuf[h, :, 512 * half : 512 * half + 512], preferred_element_type=F32)

        def swap(part, half, h):
            psend[side, part, half] = partial(h, half).astype(BF)
            p_in[side, part, half] = go.start(
                psend.at[side, part, half], precv.at[side, part, half], mate
            )

        swap(0, 0, far_h + 1 - core)
        total = partial(far_h + core, 0)
        swap(0, 1, far_h + 1 - core)
        for half in range(2):
            p_in[side, 0, half].wait_recv()
            ysend[side, half] = (total + precv[side, 0, half].astype(F32)).astype(BF)
            y_copy[side, half] = go.start(ysend.at[side, half], yrecv.at[side, half], across)
            if half == 0:
                total = partial(far_h + core, 1)
        for half in range(2):
            swap(1, half, near_h + 1 - core)
        for half in range(2):
            held[side, half] = partial(near_h + core, half)
    for side in range(2):
        for half in range(2):
            p_in[side, 1, half].wait_recv()
            y_copy[side, half].wait_recv()
            total = held[side, half] + precv[side, 1, half].astype(F32) + yrecv[side, half].astype(F32)
            out[pl.ds(128 * side, 128), pl.ds(512 * half, 512)] = total.astype(BF)

    go.wait_sends()
    pltpu.make_async_copy(drv.at[pl.ds(0, 7)], drv.at[pl.ds(0, 7)], all_send.at[0]).wait()
    pltpu.make_async_copy(frecv.at[pl.ds(0, 63)], frecv.at[pl.ds(0, 63)], all_send.at[1]).wait()
    for side in range(2):
        part = osend.at[side, pl.ds(0, 63)]
        pltpu.make_async_copy(part, part, all_send.at[2 + side]).wait()


def layer(act, w, taps, flt, w_out):
    any_space, vmem = pl.BlockSpec(memory_space=pl.ANY), pl.BlockSpec(memory_space=pltpu.VMEM)
    return pl.pallas_call(
        layer_kernel,
        out_shape=jax.ShapeDtypeStruct((BLK, 1024), BF),
        in_specs=[any_space] * 10,
        out_specs=vmem,
        scratch_shapes=[
            pltpu.VMEM((3, TAPS, 1024), F32),
            pltpu.VMEM((128, 128), BF),
            pltpu.VMEM((2, 64, BLK), F32),
            pltpu.VMEM((2 * BLK, 2 * BLK), BF),
            pltpu.VMEM((2 * BLK, 2 * BLK), BF),
            pltpu.VMEM((64, 256), BF),
            pltpu.VMEM((NY, NX, BLK, D), BF),
            pltpu.VMEM((NY, NX, NZ, DB, 3 * CG), BF),
            pltpu.VMEM((16, D), BF),
            pltpu.VMEM((16, 512), F32),
            pltpu.VMEM((16, 512), BF),
            pltpu.VMEM((NY, NX, 16, 512), BF),
            pltpu.VMEM((16, D), F32),
            pltpu.VMEM((8, 8, 3 * CG), F32),
            pltpu.VMEM((BLK + 8, 3 * CG), F32),
            pltpu.VMEM((1024, BLK), F32),
            pltpu.VMEM((8, NZ, 16, BLK), BF),
            pltpu.VMEM((64, 16, BLK), BF),
            pltpu.VMEM((NZ, 8, 16, BLK), BF),
            pltpu.VMEM((NZ, 8, 16, BLK), BF),
            pltpu.VMEM((8, CG, BLK), BF),
            pltpu.VMEM((8, CG, BLK), BF),
            pltpu.VMEM((2, 1024, 128), F32),
            pltpu.VMEM((2, 1024, 128), F32),
            pltpu.VMEM((16 // GROUP, 64 * GROUP, 2 * BLK), F32),
            pltpu.VMEM((16 // GROUP, 64 * GROUP, 2 * BLK), BF),
            pltpu.VMEM((2, 64, 16, 128), BF),
            pltpu.VMEM((2, 64, 16, 128), BF),
            pltpu.VMEM((4, 1024, 1024), BF),
            pltpu.VMEM((2, 2, 2, 128, 512), BF),
            pltpu.VMEM((2, 2, 2, 128, 512), BF),
            pltpu.VMEM((2, 2, 128, 512), BF),
            pltpu.VMEM((2, 2, 128, 512), BF),
            pltpu.VMEM((2, 2, 128, 512), F32),
            pltpu.SemaphoreType.DMA((16,)),
            pltpu.SemaphoreType.DMA((4,)),
            pltpu.SemaphoreType.DMA((4,)),
            pltpu.SemaphoreType.DMA((4,)),
            pltpu.SemaphoreType.DMA((N_COPIES,)),
            pltpu.SemaphoreType.DMA((N_COPIES,)),
        ],
        compiler_params=pltpu.CompilerParams(
            collective_id=0, has_side_effects=True, vmem_limit_bytes=58 * 1024 * 1024
        ),
        name="layer",
    )(act, w, taps, flt, w_out, *[jnp.asarray(table) for table in tables()])


def on_device(activations, w_in, short_taps, long_filter, w_out):
    return layer(activations, w_in, short_taps.transpose(0, 2, 1), long_filter, w_out)


def solution(mesh):
    return jax.shard_map(
        on_device,
        mesh=mesh,
        in_specs=(
            P("ctx", None),
            P(None, "ctx", "hid"),
            P(None, "hid", None),
            P("hid", "ctx"),
            P("hid", None),
        ),
        out_specs=P("ctx", "hid"),
        check_vma=False,
    )
```

time: 120 us -> 116 us (0.967)
  Pallas kernels: 118 us -> 114 us
    pallas_call x1, Pallas kernels: 118 us -> 114 us  [layer(): pl.pallas_call(layer_kernel, out_shape=jax.ShapeDtypeStruct((BLK, 1024),...]
where the time goes in v6:
time: 116 us
  Pallas kernels  114 us (98%)
  local copies, waits for them, and re-layouts  1.87 us (2%)
    pallas_call x1, Pallas kernels, layer(): pl.pallas_call(layer_kernel, out_shape=jax.ShapeDtypeStruct((BLK, 1024),...  114 us

profile of v6, /device:TPU:1, one launch (start us, length us, event | category | flops | bytes accessed | tf_op | source)
XLA Modules:
  0.0 116.0 jit_solution(1249730716193016300)
XLA Ops:
  0.0 114.1 %layer.1 = bf16[256,1024]{1,0:T(8,128)(2,1)} custom-call(bf16[256,4096]{1,0:T(8,128)(2,1)} %act.1, bf16[3,64,1024]{2,1,0:T(8,128)(2,1)} %w.1, f32[3,3,1024]{2,1,0:T(4,128)} %bitcast.1, f32[1024,256]{1,0:T(8,128)} %flt.1, bf16[1024,4096]{1,0:T(8,128)(2,1)} %w_out.1, bf16[128,128]{1,0:T(8,128)(2,1)} %constant.10.clone.ahead_in, ...), custom_call_target="tpu_custom_call" | custom-call | tf_op jit(solution)/shard_map/layer/pallas_call | solution.py:526
  114.1 1.9 %copy.12 = bf16[256,1024]{1,0:T(8,128)(2,1)} copy(bf16[256,1024]{1,0:T(8,128)(2,1)} %layer.1) | data formatting | bytes 1048576

commit v7 on v6

--- a/solution.py
+++ b/solution.py
@@ -20,7 +20,7 @@
 DB = 64
 
 
-HOOK = 3
+HOOK = 0
 
 
 def place():
@@ -156,6 +156,39 @@
             for j in range(3)
         ]
 
+    def a_slot(y, block, part, first_row=0, count=64):
+        return abuf.at[y, block, pl.ds(pl.multiple_of(core * 128 + part * 64 + first_row, 16), count)]
+
+    def a_send(part, to):
+        return go.start(
+            act.at[pl.ds(pl.multiple_of(core * 128 + part * 64, 64), 64)], a_slot(yl, x, part), to
+        )
+
+    y_in, mates = {}, {}
+
+    def y_send(block, dx, part, count=32):
+        for half, to in ((0, to_s), (1, to_o)):
+            piece = a_slot(yl, block, part, half * count, count)
+            y_in[dx, part, half] = go.start(piece, piece, to)
+
+    def mate_own(block, dx, part):
+        mates[0, dx, part] = go.start(a_slot(yl, block, part), a_slot(yl, block, part), mate)
+
+    def mate_other(block, dx, part):
+        y_in[dx, part, 0].wait_recv()
+        y_in[dx, part, 1].wait_recv()
+        if dx == 2:
+            far_other[part].wait_recv()
+        mates[1, dx, part] = go.start(a_slot(1 - yl, block, part), a_slot(1 - yl, block, part), mate)
+
+    near = [a_send(0, to_xr), a_send(1, to_xl)]
+    for part in range(2):
+        for half, to in ((0, to_s), (1, to_o)):
+            begin = pl.multiple_of(core * 128 + part * 64 + half * 32, 32)
+            y_in[0, part, half] = go.start(
+                act.at[pl.ds(begin, 32)], a_slot(yl, x, part, half * 32, 32), to
+            )
+
     def send(unit, zs, to):
         yu, xu = rel(*unit)
         part = wbuf.at[yu, xu, zs]
@@ -196,35 +229,6 @@
             copy.wait_recv()
         send_own(unit)
 
-    def a_slot(y, block, part, first_row=0, count=64):
-        return abuf.at[y, block, pl.ds(pl.multiple_of(core * 128 + part * 64 + first_row, 16), count)]
-
-    def a_send(part, to):
-        return go.start(
-            act.at[pl.ds(pl.multiple_of(core * 128 + part * 64, 64), 64)], a_slot(yl, x, part), to
-        )
-
-    y_in, mates = {}, {}
-
-    def y_send(block, dx, part, count=32):
-        for half, to in ((0, to_s), (1, to_o)):
-            piece = a_slot(yl, block, part, half * count, count)
-            y_in[dx, part, half] = go.start(piece, piece, to)
-
-    def mate_own(block, dx, part):
-        mates[0, dx, part] = go.start(a_slot(yl, block, part), a_slot(yl, block, part), mate)
-
-    def mate_other(block, dx, part):
-        y_in[dx, part, 0].wait_recv()
-        y_in[dx, part, 1].wait_recv()
-        if dx == 2:
-            far_other[part].wait_recv()
-        mates[1, dx, part] = go.start(a_slot(1 - yl, block, part), a_slot(1 - yl, block, part), mate)
-
-    near = [a_send(0, to_xr), a_send(1, to_xl)]
-    own_a.wait()
-    y_send(x, 0, 0)
-    y_send(x, 0, 1)
     for copy in loads:
         copy.wait()
     f16buf[...] = f32buf[...].astype(BF).reshape(8, NZ, 16, BLK)
@@ -238,6 +242,8 @@
             from_r[unit, step].wait_recv()
             if step < 3 or k % 2 == 1:
                 from_r[unit, step + 1] = send(unit, zr, to_l)
+            if step == 1 and k == 4:
+                near.extend([a_send(1, to_xr), a_send(0, to_xl)])
             if k == HOOK and step in hooks:
                 hooks[step]()
 
@@ -260,8 +266,8 @@
         mate_own(xr, 1, 0)
 
     far, far_other, hooks = [], [], {2: first_halves, 3: second_halves}
+    own_a.wait()
     relay(1)
-    near += [a_send(1, to_xr), a_send(0, to_xl)]
     for copy in own_o:
         copy.start()
     relay(2)

time: 116 us -> 113 us (0.974)
  Pallas kernels: 114 us -> 111 us
    pallas_call x1, Pallas kernels: 114 us -> 111 us  [layer(): pl.pallas_call(layer_kernel, out_shape=jax.ShapeDtypeStruct((BLK, 1024),...]
where the time goes in v7:
time: 113 us
  Pallas kernels  111 us (98%)
  local copies, waits for them, and re-layouts  1.87 us (2%)
    pallas_call x1, Pallas kernels, layer(): pl.pallas_call(layer_kernel, out_shape=jax.ShapeDtypeStruct((BLK, 1024),...  111 us

profile of v7, /device:TPU:1, one launch (start us, length us, event | category | flops | bytes accessed | tf_op | source)
XLA Modules:
  0.0 112.6 jit_solution(4966106496477773273)
XLA Ops:
  0.0 110.7 %layer.1 = bf16[256,1024]{1,0:T(8,128)(2,1)} custom-call(bf16[256,4096]{1,0:T(8,128)(2,1)} %act.1, bf16[3,64,1024]{2,1,0:T(8,128)(2,1)} %w.1, f32[3,3,1024]{2,1,0:T(4,128)} %bitcast.1, f32[1024,256]{1,0:T(8,128)} %flt.1, bf16[1024,4096]{1,0:T(8,128)(2,1)} %w_out.1, bf16[128,128]{1,0:T(8,128)(2,1)} %constant.10.clone.ahead_in, ...), custom_call_target="tpu_custom_call" | custom-call | tf_op jit(solution)/shard_map/layer/pallas_call | solution.py:532
  110.7 1.9 %copy.12 = bf16[256,1024]{1,0:T(8,128)(2,1)} copy(bf16[256,1024]{1,0:T(8,128)(2,1)} %layer.1) | data formatting | bytes 1048576

commit v8 on v7

--- a/solution.py
+++ b/solution.py
@@ -79,12 +79,11 @@
     wide = wide[sides][:, sides]
     ahead_h, ahead_l = halves(ahead[:, order])
     back_h, back_l = halves(back[order])
-    wide_h, wide_l = halves(wide)
+    wide_h, _ = halves(wide)
     return (
         np.concatenate([ahead_h, ahead_l], axis=1),
         np.stack([np.cos(turn), -np.sin(turn)]).astype(np.float32),
         wide_h,
-        wide_l,
         np.concatenate([back_h, back_l], axis=1),
     )
 
@@ -100,12 +99,12 @@
 
 
 def layer_kernel(
-    act, w, taps_in, flt, w_out, ahead_in, turn_in, wide_h_in, wide_l_in, back_in, out,
-    taps, ahead, turn, wide_h, wide_l, back, abuf, wbuf, last16, packed, halo_out, halo_in, halo_act, halo_br, bs, f32buf, f16buf, frecv, drv, drecv, qry, qrecv, wide, out32, spec, prod, osend, crecv,
+    act, w, taps_in, flt, w_out, ahead_in, turn_in, wide_h_in, back_in, out,
+    taps, ahead, turn, wide_h, back, abuf, wbuf, last16, packed, halo_out, halo_in, halo_act, halo_br, bs, f32buf, f16buf, frecv, drv, drecv, qry, qrecv, wide, out32, spec, prod, osend, crecv,
     obuf, psend, precv, ysend, yrecv, held, local_sem, own_sem, all_send, all_recv, send_sem, recv_sem,
 ):
     tables_here = (
-        (taps_in, taps), (ahead_in, ahead), (turn_in, turn), (wide_h_in, wide_h), (wide_l_in, wide_l), (back_in, back)
+        (taps_in, taps), (ahead_in, ahead), (turn_in, turn), (wide_h_in, wide_h), (back_in, back)
     )
     ctx, hid, yl, x, z = place()
     core = lax.rem(hid, 2)
@@ -242,7 +241,7 @@
             from_r[unit, step].wait_recv()
             if step < 3 or k % 2 == 1:
                 from_r[unit, step + 1] = send(unit, zr, to_l)
-            if step == 1 and k == 4:
+            if step == 1 and k == 1:
                 near.extend([a_send(1, to_xr), a_send(0, to_xl)])
             if k == HOOK and step in hooks:
                 hooks[step]()
@@ -273,13 +272,6 @@
     relay(2)
     mate_other(x, 0, 0)
     mate_other(x, 0, 1)
-    for copy in halos:
-        copy.wait_recv()
-    for y in range(NY):
-        for xs in range(NX):
-            got = halo_in[y, xs].astype(F32)
-            for k in range(8):
-                halo_act[pl.ds(2 * (y * NX + xs), 2), pl.ds(512 * k, 512)] = got[2 * k : 2 * k + 2]
     relay(3)
     mate_other(xl, 3, 0)
     mate_other(xr, 1, 1)
@@ -314,6 +306,14 @@
     own_f = to_owners(lambda yt, xt, zt: f16buf.at[xt * NY + yt, zt], frecv.at[here], 1)
     for k, unit in enumerate(PLANE):
         (from_l if k % 2 == 0 else from_r)[unit, 4].wait_recv()
+    for copy in halos:
+        copy.wait_recv()
+    for y in range(NY):
+        for xs in range(NX):
+            got = halo_in[y, xs].astype(F32)
+            for k in range(8):
+                halo_act[pl.ds(2 * (y * NX + xs), 2), pl.ds(512 * k, 512)] = got[2 * k : 2 * k + 2]
+
     def await_mates(keys):
         for key in keys:
             for part in range(2):
@@ -366,12 +366,12 @@
         return carry
 
     await_mates([(0, 1), (0, 3), (1, 0)])
-    lax.fori_loop(0, 2, early, 0)
+    lax.fori_loop(0, 3, early, 0)
     for part in range(2):
         far[part].wait_recv()
         y_send(xo, 2, part, 16)
         mate_own(xo, 2, part)
-    lax.fori_loop(2, 4, early, 0)
+    lax.fori_loop(3, 4, early, 0)
 
 
     mate_other(xl, 3, 1)
@@ -417,12 +417,7 @@
         return jnp.concatenate(parts, axis=0)
 
     def filter_group(g, carry):
-        high, low = split(turned(g * GROUP))
-        spec[g] = (
-            inner(high, slice(None))
-            + inner(low, slice(None))
-            + jnp.dot(high, wide_l[...], preferred_element_type=F32)
-        )
+        spec[g] = inner(turned(g * GROUP).astype(BF), slice(None))
         return carry
 
     def signal_group(g, carry):
@@ -532,13 +527,12 @@
     return pl.pallas_call(
         layer_kernel,
         out_shape=jax.ShapeDtypeStruct((BLK, 1024), BF),
-        in_specs=[any_space] * 10,
+        in_specs=[any_space] * 9,
         out_specs=vmem,
         scratch_shapes=[
             pltpu.VMEM((3, TAPS, 1024), F32),
             pltpu.VMEM((128, 128), BF),
             pltpu.VMEM((2, 64, BLK), F32),
-            pltpu.VMEM((2 * BLK, 2 * BLK), BF),
             pltpu.VMEM((2 * BLK, 2 * BLK), BF),
             pltpu.VMEM((64, 256), BF),
             pltpu.VMEM((NY, NX, BLK, D), BF),

time: 113 us -> 112 us (level)
  no operation moved by 1% of the time
where the time goes in v8:
time: 112 us
  Pallas kernels  110 us (98%)
  local copies, waits for them, and re-layouts  1.87 us (2%)
    pallas_call x1, Pallas kernels, layer(): pl.pallas_call(layer_kernel, out_shape=jax.ShapeDtypeStruct((BLK, 1024),...  110 us

profile of v8, /device:TPU:1, one launch (start us, length us, event | category | flops | bytes accessed | tf_op | source)
XLA Modules:
  0.0 112.0 jit_solution(10242841107260355587)
XLA Ops:
  0.0 110.1 %layer.1 = bf16[256,1024]{1,0:T(8,128)(2,1)} custom-call(bf16[256,4096]{1,0:T(8,128)(2,1)} %act.1, bf16[3,64,1024]{2,1,0:T(8,128)(2,1)} %w.1, f32[3,3,1024]{2,1,0:T(4,128)} %bitcast.1, f32[1024,256]{1,0:T(8,128)} %flt.1, bf16[1024,4096]{1,0:T(8,128)(2,1)} %w_out.1, bf16[128,128]{1,0:T(8,128)(2,1)} %constant.8.clone.ahead_in, ...), custom_call_target="tpu_custom_call" | custom-call | tf_op jit(solution)/shard_map/layer/pallas_call | solution.py:527
  110.1 1.9 %copy.11 = bf16[256,1024]{1,0:T(8,128)(2,1)} copy(bf16[256,1024]{1,0:T(8,128)(2,1)} %layer.1) | data formatting | bytes 1048576
